TPU v7x, 32 devices: a whole 2x2x4 slice. The times are simulated.
32 devices in a mesh: groups: 2 (over y), clus: 4 (over z), tp: 2 (over x), rep: 2 (over core).
Axes of the slice: x: 2, y: 2, z: 4, core: 2. Of those that a mesh axis runs over, the one named last changes fastest.
Arguments:
- hidden: bfloat16 [3072, 8192], P(('groups', 'clus'), ('tp', 'rep')), parts along dimension 0, may hold values from -6 to 6
- residual: bfloat16 [3072, 4096], P(('groups', 'clus'), ('tp', 'rep')), parts along dimension 0, may hold values from -6 to 6
- down_weight: bfloat16 [8192, 4096], P(('tp', 'rep'), 'clus'), may hold values from -0.0625 to 0.0625
- norm_gain: float32 [4096], P(('tp', 'rep')), may hold values from 0.1 to 1.9
- cluster_id: int32 [3072, 1], P(('groups', 'clus')), parts along dimension 0, may hold values from 0 to 23, as said below
Outputs:
- embedded: bfloat16 [3072, 4096], P(('groups', 'clus'), ('tp', 'rep')), parts along dimension 0
- score: float32 [3072], P(('groups', 'clus')), parts along dimension 0
There are 2 independent parts, one for each index of `groups`. A program takes and returns all parts, laid end to end along the dimension named above; an argument that names none is the same for every part. Nothing has to cross between parts.
Inputs may be any that keep to these rules, and one draw needn't show every extreme that they name: `cluster_id`: the rows of one device name each cluster at most 32 times; one cluster is named exactly 32 times by the rows of every device.
All inputs are finite; a program needn't handle non-finite values.
Results may differ from a plain program's by a relative error of at most 0.0095.
Values may be sent and summed in bfloat16 or wider, within the bound.
No kernel may reach another device: no remote copies, remote signals or barrier semaphores. Data moves between devices by JAX's collectives and lax.ppermute only.
A program may use at most 128 MiB of HBM per device.

v0:
```python
import jax
import jax.numpy as jnp
from jax import lax
from jax.sharding import PartitionSpec as P

D = 4096
CL_OWN = 6


EPS = 1e-06


def best_match(block, valid):
    slots = block.shape[2]
    row_index = jnp.arange(block.shape[1], dtype=jnp.int32)
    col_index = jnp.arange(slots, dtype=jnp.int32)
    keep = valid[:, None, :] & (row_index[:, None] != col_index[None, :])[None, :, :]
    best = jnp.max(jnp.where(keep, block, jnp.float32(-4.0)), axis=2)
    found = jnp.any(keep, axis=2)
    return jnp.where(found, D**0.5 * best, jnp.float32(-1.0))


def per_device(hidden, residual, down_weight, norm_gain, cluster_id):
    rows = hidden.shape[0]
    owners = lax.axis_size("clus")
    per_owner = CL_OWN
    clusters = per_owner * owners
    capacity = 2 * rows // clusters
    span = owners * capacity
    terms = jnp.dot(
        hidden,
        lax.all_gather(down_weight, "clus", axis=1, tiled=True),
        preferred_element_type=jnp.float32,
    )
    summed = lax.psum_scatter(
        terms.astype(jnp.bfloat16), ("tp", "rep"), scatter_dimension=1, tiled=True
    ).astype(jnp.float32)
    scaled = (summed + residual.astype(jnp.float32)) * norm_gain[None, :]
    total = lax.psum(jnp.sum(scaled * scaled, axis=1), ("tp", "rep"))
    embedded = (scaled * lax.rsqrt(total + EPS)[:, None]).astype(jnp.bfloat16)
    labels = cluster_id[:, 0]
    owner = labels // per_owner
    local = labels % per_owner
    positions = jnp.arange(rows, dtype=jnp.int32)
    earlier = (labels[:, None] == labels[None, :]) & (positions[None, :] < positions[:, None])
    rank = jnp.sum(earlier.astype(jnp.int32), axis=1)
    target = local * span + owner * capacity + rank
    placing = jnp.arange(per_owner * span, dtype=jnp.int32)[:, None] == target[None, :]
    outgoing = jnp.dot(
        placing.astype(jnp.bfloat16), embedded, preferred_element_type=jnp.float32
    ).astype(jnp.bfloat16)
    outgoing = outgoing.reshape(per_owner, span, embedded.shape[1])
    present = (
        jnp.sum(placing.astype(jnp.float32), axis=1).astype(jnp.bfloat16).reshape(per_owner, span)
    )
    arrived, filled = (
        lax.all_to_all(outgoing, "clus", split_axis=1, concat_axis=1, tiled=True),
        lax.all_to_all(present, "clus", split_axis=1, concat_axis=1, tiled=True),
    )
    partial_value = jnp.einsum("ksd,ktd->kst", arrived, arrived, preferred_element_type=jnp.float32)
    valid = filled > 0
    gram = lax.psum(partial_value.astype(jnp.bfloat16), ("tp", "rep")).astype(jnp.float32)
    best = best_match(gram, valid)
    returned = lax.all_to_all(best, "clus", split_axis=1, concat_axis=1, tiled=True)
    score = jnp.sum(jnp.where(placing, returned.reshape(-1)[:, None], jnp.float32(0.0)), axis=0)
    return (embedded, score)


def solution(mesh):
    return jax.shard_map(
        per_device,
        mesh=mesh,
        in_specs=(
            P(("groups", "clus"), ("tp", "rep")),
            P(("groups", "clus"), ("tp", "rep")),
            P(("tp", "rep"), "clus"),
            P(("tp", "rep")),
            P(("groups", "clus"), None),
        ),
        out_specs=(P(("groups", "clus"), ("tp", "rep")), P(("groups", "clus"))),
        check_vma=False,
    )
```

profile of v0, /device:TPU:0, one launch (start us, length us, event | category | flops | bytes accessed | tf_op | source)
XLA Modules:
  0.0 466.0 jit_solution(10569333358309845739)
XLA Ops:
  7.2 0.0 copy-start
  7.2 0.0 all-gather.2.cloned.1.call-start
  7.2 0.7 all-gather.2.cloned.1.call-update
  7.9 0.0 reduce-scatter.2.cloned.1.call-start
  8.0 291.1 %all-gather.2.cloned.1.call-done = bf16[2048,4096]{1,0:T(8,128)(2,1)} async-done(((bf16[2048,1024]{1,0:T(8,128)(2,1)}), bf16[2048,4096]{1,0:T(8,128)(2,1)}) %all-gather.2.cloned.1.call-update) | async-done | bytes 16777232 | tf_op jit(solution)/shard_map/all_gather | solution.py:32
  299.1 0.0 copy-done
  299.1 11.4 %convolution_convert_fusion = bf16[384,4096]{1,0:T(8,128)(2,1)} fusion(bf16[384,2048]{1,0:T(8,128)(2,1)S(1)} %copy-done, bf16[2048,4096]{1,0:T(8,128)(2,1)} %all-gather.2.cloned.1.call-done), kind=kOutput, calls=%fused_computation | convolution fusion | flops 6444023808 | bytes 21495808 | tf_op jit(solution)/shard_map/dot_general | solution.py:30
  310.5 0.0 copy-start.5
  310.5 0.0 copy-start.1
  310.5 0.0 copy-start.4
  310.5 0.0 reduce-scatter.2.cloned.1.call-update
  310.5 0.7 copy-done.5
  311.2 0.2 convert_reduce_fusion.1
  311.4 0.2 convert_reduce_fusion
  311.6 0.1 convert_element_type.43
  311.7 0.6 copy.24
  312.3 3.2 all-to-all-start
  315.6 31.2 %reduce-scatter.2.cloned.1.call-done = bf16[384,1024]{1,0:T(8,128)(2,1)} async-done(((bf16[384,4096]{1,0:T(8,128)(2,1)}), bf16[384,1024]{1,0:T(8,128)(2,1)}) %reduce-scatter.2.cloned.1.call-update) | async-done | bytes 786448 | tf_op jit(solution)/shard_map/reduce_scatter | solution.py:35
  346.8 0.0 copy-done.1
  346.8 0.0 copy-done.4
  346.8 0.0 copy-start.2
  346.8 1.6 multiply_reduce_fusion
  348.4 5.8 %psum.14 = f32[384]{0:T(512)S(1)} all-reduce(f32[384]{0:T(512)S(1)} %multiply_reduce_fusion), channel_id=1, replica_groups=mesh['groups'=2,'clus'=4,'tp'=2,'rep'=2] {'tp','rep'}, use_global_device_ids=true, to_apply=%region_2.0 | all-reduce | flops 384 | bytes 3072 | tf_op jit(solution)/shard_map/psum | solution.py:39
  354.2 0.0 copy-done.2
  354.2 0.3 multiply_convert_fusion
  354.5 0.0 copy-start.3
  354.5 0.9 copy-done.3
  355.4 1.0 convolution_convert_fusion.1
  356.4 2.2 copy.26
  358.5 0.0 all-to-all-done
  358.5 4.8 %all-to-all-start.1 = ((bf16[6,128,1024]{2,0,1:T(8,128)(2,1)}), bf16[6,128,1024]{2,0,1:T(8,128)(2,1)}, u32[]{:S(2)}, u32[]{:S(2)}) async-start(bf16[6,128,1024]{2,0,1:T(8,128)(2,1)} %copy.26), calls=%async_computation.2 | async-start | bytes 4194304 | tf_op jit(solution)/shard_map/all_to_all | solution.py:57
  363.3 0.0 all-reduce.2.cloned.1.call-start
  363.3 0.1 gt.15
  363.4 48.0 %all-to-all-done.1 = bf16[6,128,1024]{2,0,1:T(8,128)(2,1)} async-done(((bf16[6,128,1024]{2,0,1:T(8,128)(2,1)}), bf16[6,128,1024]{2,0,1:T(8,128)(2,1)}, u32[]{:S(2)}, u32[]{:S(2)}) %all-to-all-start.1) | async-done | bytes 1572896 | tf_op jit(solution)/shard_map/all_to_all | solution.py:57
  411.5 4.7 %fusion.2 = bf16[6,128,128]{2,1,0:T(8,128)(2,1)} fusion(bf16[6,128,1024]{2,0,1:T(8,128)(2,1)} %all-to-all-done.1), kind=kOutput, calls=%fused_computation.10 | convolution fusion | flops 201424896 | bytes 1769472 | tf_op jit(solution)/shard_map/ksd,ktd->kst/dot_general | solution.py:60
  416.2 0.0 all-reduce.2.cloned.1.call-update
  416.2 0.2 and_reduce_fusion
  416.4 29.8 %all-reduce.2.cloned.1.call-done = bf16[6,128,128]{2,1,0:T(8,128)(2,1)} async-done(((bf16[6,128,128]{2,1,0:T(8,128)(2,1)}), bf16[6,128,128]{2,1,0:T(8,128)(2,1)}) %all-reduce.2.cloned.1.call-update) | async-done | bytes 196624 | tf_op jit(solution)/shard_map/psum | solution.py:62
  446.2 1.1 fusion.7
  447.2 0.1 select_n.40
  447.3 0.1 reshape.75
  447.4 10.0 %all_to_all.17 = f32[4,1,192]{2,1,0:T(1,128)S(1)} all-to-all(f32[4,1,192]{2,1,0:T(1,128)S(1)} %reshape.75), channel_id=1, replica_groups=mesh['groups'=2,'clus'=4,'tp'=2,'rep'=2] {'clus'}, dimensions={0} | all-to-all | bytes 6144 | tf_op jit(solution)/shard_map/all_to_all | solution.py:64
  457.4 0.5 broadcast.63
  457.9 0.7 reduce.1
  458.5 0.1 reshape.76
  458.6 0.1 broadcast_in_dim.34
  458.7 0.8 select_reduce_fusion
  (9 shorter events, 0.1 us)
Async XLA Ops:
  7.2 291.9 %copy-start = (bf16[384,2048]{1,0:T(8,128)(2,1)S(1)}, bf16[384,2048]{1,0:T(8,128)(2,1)}, u32[]{:S(2)}) copy-start(bf16[384,2048]{1,0:T(8,128)(2,1)} %param.5) | copy-start | bytes 4718596
  7.2 291.9 %all-gather.2.cloned.1.call-start = ((), (), s32[]{:S(2)}) async-start(), calls=%async_computation.4 | async-start | bytes 20971520 | tf_op jit(solution)/shard_map/all_gather | solution.py:32
  7.9 338.9 %reduce-scatter.2.cloned.1.call-start = ((), (), s32[]{:S(2)}) async-start(), calls=%async_computation.5 | async-start | bytes 3932160 | tf_op jit(solution)/shard_map/reduce_scatter | solution.py:35
  310.5 0.7 copy-start.5
  310.5 36.3 %copy-start.1 = (bf16[384,1024]{1,0:T(8,128)(2,1)S(1)}, bf16[384,1024]{1,0:T(8,128)(2,1)}, u32[]{:S(2)}) copy-start(bf16[384,1024]{1,0:T(8,128)(2,1)} %param.6) | copy-start | bytes 2359300
  310.5 36.3 %copy-start.4 = (f32[1024]{0:T(1024)S(1)}, f32[1024]{0:T(1024)}, u32[]{:S(2)}) copy-start(f32[1024]{0:T(1024)} %param.8) | copy-start | bytes 12292
  312.3 46.2 %all-to-all-start = ((bf16[6,4,32]{2,0,1:T(8,128)(2,1)}), bf16[6,4,32]{2,0,1:T(8,128)(2,1)S(1)}, u32[]{:S(2)}, u32[]{:S(2)}) async-start(bf16[6,4,32]{2,0,1:T(8,128)(2,1)} %copy.24), calls=%async_computation.1 | async-start | bytes 16384 | tf_op jit(solution)/shard_map/all_to_all | solution.py:58
  346.8 7.4 %copy-start.2 = (bf16[384,1024]{1,0:T(8,128)(2,1)S(1)}, bf16[384,1024]{1,0:T(8,128)(2,1)}, u32[]{:S(2)}) copy-start(bf16[384,1024]{1,0:T(8,128)(2,1)} %reduce-scatter.2.cloned.1.call-done) | copy-start | bytes 2359300
  354.5 0.9 copy-start.3
  358.5 52.9 %all-to-all-start.1 = ((bf16[6,128,1024]{2,0,1:T(8,128)(2,1)}), bf16[6,128,1024]{2,0,1:T(8,128)(2,1)}, u32[]{:S(2)}, u32[]{:S(2)}) async-start(bf16[6,128,1024]{2,0,1:T(8,128)(2,1)} %copy.26), calls=%async_computation.2 | async-start | bytes 4194304 | tf_op jit(solution)/shard_map/all_to_all | solution.py:57
  363.3 82.9 %all-reduce.2.cloned.1.call-start = ((), (), s32[]{:S(2)}) async-start(), calls=%async_computation.6 | async-start | bytes 393216 | tf_op jit(solution)/shard_map/psum | solution.py:62
Sparse Core Ops, SparseCore 0:
  9.6 289.4 all-gather.1
  310.6 36.1 reduce-scatter.1
  416.3 29.8 all-reduce.1
where the time goes:
time: 466 us
  waiting for transfers between devices  401 us (86%)
  matrix products  17 us (4%)
  blocking collectives  15.7 us (3%)
  between operations  13.8 us (3%)
  starting transfers between devices  8.07 us (2%)
  local copies, waits for them, and re-layouts  5.35 us (1%)
  other arithmetic  5.12 us (1%)
    all_gather x1, waiting for transfers between devices, per_device(): lax.all_gather(down_weight, 'clus', axis=1, tiled=True)  291 us
    all_to_all x1, waiting for transfers between devices, per_device(): lax.all_to_all(outgoing, 'clus', split_axis=1, concat_axis=1, tiled=True)  48 us
    reduce_scatter x1, waiting for transfers between devices, per_device(): lax.psum_scatter(terms.astype(jnp.bfloat16), ('tp', 'rep'), scatter_dimen...  31.2 us
    psum x1, waiting for transfers between devices, per_device(): lax.psum(partial_value.astype(jnp.bfloat16), ('tp', 'rep'))  29.8 us
    dot_general x1, matrix products, per_device(): jnp.dot(hidden, lax.all_gather(down_weight, 'clus', axis=1, tiled=True),...  11.4 us
    all_to_all x1, blocking collectives, per_device(): lax.all_to_all(best, 'clus', split_axis=1, concat_axis=1, tiled=True)  9.96 us
  transfers between devices with their start and end apart: 5, of which 4 were waited for; matrix products, arithmetic and copies ran while one was open for 1% of the time, Pallas kernels for 0%

commit v1 on v0

--- a/solution.py
+++ b/solution.py
@@ -1,13 +1,14 @@
 import jax
 import jax.numpy as jnp
 from jax import lax
+from jax.experimental import pallas as pl
+from jax.experimental.pallas import tpu as pltpu
 from jax.sharding import PartitionSpec as P
 
 D = 4096
 CL_OWN = 6
-
-
 EPS = 1e-06
+F32, BF16 = jnp.float32, jnp.bfloat16
 
 
 def best_match(block, valid):
@@ -20,7 +21,7 @@
     return jnp.where(found, D**0.5 * best, jnp.float32(-1.0))
 
 
-def per_device(hidden, residual, down_weight, norm_gain, cluster_id):
+def any_mesh(hidden, residual, down_weight, norm_gain, cluster_id):
     rows = hidden.shape[0]
     owners = lax.axis_size("clus")
     per_owner = CL_OWN
@@ -66,9 +67,369 @@
     return (embedded, score)
 
 
+OUT_IN = [(0, 1), (3, 2)]
+IN_OUT = [(1, 0), (2, 3)]
+IN_IN = [(1, 2), (2, 1)]
+FAR_IN = [(0, 2), (3, 1)]
+SWAP = [(0, 1), (1, 0)]
+CHUNKS = 4
+
+
+def after(value, *earlier):
+    return lax.optimization_barrier((value, *earlier))[0] if earlier else value
+
+
+def zc(pairs):
+    return [(a * 2 + b, c * 2 + d) for (a, b), (c, d) in pairs]
+
+
+FREE = pl.CostEstimate(flops=1024, bytes_accessed=1024, transcendentals=0)
+
+
+def late_part(y, rows, own, other, which=0):
+    every, depth = rows.shape
+    cols = other.shape[1]
+    block = every // 2
+
+    def body(_, a, b, own, other, out):
+        total = jnp.dot(a[...], own[...], preferred_element_type=F32)
+        total = total + jnp.dot(b[...], other[...], preferred_element_type=F32)
+        out[...] = total.astype(BF16)
+
+    return pl.pallas_call(
+        body,
+        grid_spec=pltpu.PrefetchScalarGridSpec(
+            num_scalar_prefetch=1,
+            grid=(every // block,),
+            in_specs=[
+                pl.BlockSpec((block, depth // 2), lambda i, y: (i, y[0])),
+                pl.BlockSpec((block, depth // 2), lambda i, y: (i, 1 - y[0])),
+                pl.BlockSpec((depth // 2, cols), lambda i, y: (0, which)),
+                pl.BlockSpec((depth // 2, cols), lambda i, y: (0, 0)),
+            ],
+            out_specs=pl.BlockSpec((block, cols), lambda i, y: (i, 0)),
+        ),
+        out_shape=jax.ShapeDtypeStruct((every, cols), BF16),
+        compiler_params=pltpu.CompilerParams(vmem_limit_bytes=24 * 2**20),
+        cost_estimate=FREE,
+        name="late_part",
+    )(jnp.asarray(y, jnp.int32).reshape(1), rows, rows, own, other)
+
+
+def product(rows, w):
+    m, depth = rows.shape
+    cols = w.shape[1]
+    block = 256
+
+    def body(a, b, out):
+        out[...] = jnp.dot(a[...], b[...], preferred_element_type=F32).astype(BF16)
+
+    return pl.pallas_call(
+        body,
+        grid=(cols // block,),
+        in_specs=[
+            pl.BlockSpec((m, depth), lambda i: (0, 0)),
+            pl.BlockSpec((depth, block), lambda i: (0, i)),
+        ],
+        out_specs=pl.BlockSpec((m, block), lambda i: (0, i)),
+        out_shape=jax.ShapeDtypeStruct((m, cols), BF16),
+        compiler_params=pltpu.CompilerParams(vmem_limit_bytes=24 * 2**20),
+        cost_estimate=FREE,
+        name="product",
+    )(rows, w)
+
+
+def fold(x, part, met):
+    rows, cols = part.shape
+    width = cols // 2
+    block = 384
+
+    def body(_, a, b, c, d, keep, give):
+        keep[...] = a[...].astype(F32) + b[...].astype(F32)
+        give[...] = (c[...].astype(F32) + d[...].astype(F32)).astype(BF16)
+
+    kept = pl.BlockSpec((block, width), lambda i, x: (i, x[0]))
+    given = pl.BlockSpec((block, width), lambda i, x: (i, 1 - x[0]))
+    out = pl.BlockSpec((block, width), lambda i, x: (i, 0))
+    return pl.pallas_call(
+        body,
+        grid_spec=pltpu.PrefetchScalarGridSpec(
+            num_scalar_prefetch=1,
+            grid=(rows // block,),
+            in_specs=[kept, kept, given, given],
+            out_specs=[out, out],
+        ),
+        out_shape=[
+            jax.ShapeDtypeStruct((rows, width), F32),
+            jax.ShapeDtypeStruct((rows, width), BF16),
+        ],
+        compiler_params=pltpu.CompilerParams(vmem_limit_bytes=24 * 2**20),
+        cost_estimate=FREE,
+        name="fold",
+    )(jnp.asarray(x, jnp.int32).reshape(1), part, met, part, met)
+
+
+def tile_gram(is_late, place, late, early):
+    every, width = late.shape
+    tile = 128
+    tiles = every // tile
+
+    def body(flag, place, late, early, gram, squares, rows):
+        rows[every:, :] = jnp.zeros((tile, width), BF16)
+        value = jnp.where(flag[0] == 1, late[...], early[...])
+        at = jax.lax.broadcasted_iota(jnp.int32, (tile, every), 0)
+        for t in range(tiles):
+            one = (at + t * tile == place[...]).astype(F32).astype(BF16)
+            rows[t * tile : (t + 1) * tile, :] = jnp.dot(
+                one, value, preferred_element_type=F32
+            ).astype(BF16)
+        i = jax.lax.broadcasted_iota(jnp.int32, (tile, tile), 0)
+        j = jax.lax.broadcasted_iota(jnp.int32, (tile, tile), 1)
+        for t in range(tiles):
+            product = jax.lax.dot_general(
+                rows[t * tile : (t + 1) * tile, :],
+                rows[t * tile : (t + 2) * tile, :],
+                (((1,), (1,)), ((), ())),
+                preferred_element_type=F32,
+            )
+            gram[t] = product.astype(BF16)
+            squares[t : t + 1, :] = jnp.sum(
+                jnp.where(i == j, product[:, :tile], 0.0), axis=0, keepdims=True
+            )
+
+    return pl.pallas_call(
+        body,
+        grid_spec=pltpu.PrefetchScalarGridSpec(
+            num_scalar_prefetch=1,
+            grid=(1,),
+            in_specs=[
+                pl.BlockSpec((1, every), lambda i, f: (0, 0)),
+                pl.BlockSpec((every, width), lambda i, f: (0, 0)),
+                pl.BlockSpec((every, width), lambda i, f: (0, 0)),
+            ],
+            out_specs=[
+                pl.BlockSpec((tiles, tile, 2 * tile), lambda i, f: (0, 0, 0)),
+                pl.BlockSpec((tiles, tile), lambda i, f: (0, 0)),
+            ],
+            scratch_shapes=[pltpu.VMEM((every + tile, width), BF16)],
+        ),
+        out_shape=[
+            jax.ShapeDtypeStruct((tiles, tile, 2 * tile), BF16),
+            jax.ShapeDtypeStruct((tiles, tile), F32),
+        ],
+        compiler_params=pltpu.CompilerParams(vmem_limit_bytes=24 * 2**20),
+        cost_estimate=FREE,
+        name="tile_gram",
+    )(jnp.asarray(is_late, jnp.int32).reshape(1), place.reshape(1, every), late, early)
+
+
+def line_of_four(hidden, residual, down_weight, norm_gain, cluster_id):
+    rows, depth = hidden.shape
+    cols = down_weight.shape[1]
+    half = cols // 2
+    q = half // CHUNKS
+    every = 4 * rows
+    y, z, x, c = (lax.axis_index(a) for a in ("groups", "clus", "tp", "rep"))
+    side = z // 2
+    inner = (z == 1) | (z == 2)
+
+    early_core = zc([((1, 0), (1, 1)), ((2, 1), (2, 0))])
+    late_core = zc([((1, 1), (1, 0)), ((2, 0), (2, 1))])
+    early_x = [(5, 7), (7, 5), (8, 10), (10, 8)]
+    late_x = [(4, 6), (6, 4), (9, 11), (11, 9)]
+
+    def over_rep(part, pairs):
+        return fold(x, part, lax.ppermute(part, ("clus", "rep"), pairs))
+
+    def over_tp(keep, give, pairs):
+        return keep + lax.ppermute(give, ("clus", "tp", "rep"), pairs).astype(F32)
+
+    def across(value, *gates):
+        return lax.ppermute(after(value, *gates), "groups", SWAP)
+
+    def inward(value, *gates):
+        return lax.ppermute(after(value, *gates), "clus", OUT_IN)
+
+    stage = lax.optimization_barrier
+    names = cluster_id[:, 0]
+    h_outer = inward(hidden)
+    h_other = lax.ppermute(hidden, "clus", IN_IN)
+    names = jnp.concatenate(
+        [names] + [lax.ppermute(names, "clus", pairs) for pairs in (OUT_IN, IN_IN, FAR_IN)]
+    )
+    mine = lax.dynamic_slice_in_dim(residual, x * half, half, 1)
+    theirs = lax.dynamic_slice_in_dim(residual, (1 - x) * half, half, 1)
+    w_half = lax.dynamic_slice_in_dim(down_weight, y * (depth // 2), depth // 2, 0)
+    taken = lambda j, n: [w_half[:, i * half + j * q : i * half + (j + n) * q] for i in range(2)]
+    pieces = [jnp.concatenate(v, axis=1) for v in (taken(0, 2), taken(2, 2))]
+    part = product(hidden, down_weight)
+
+    h_outer, h_other, names, part, pieces, theirs = stage(
+        (h_outer, h_other, names, part, pieces, theirs)
+    )
+    got0 = inward(pieces[0])
+    top = rows // 2
+    far0 = lax.ppermute(h_outer[:top], "clus", IN_IN)
+    came = lax.ppermute(theirs, "tp", SWAP)
+    gain_other = lax.ppermute(norm_gain, "tp", SWAP)
+    first = []
+    part = [part] + [product(after(v, came), down_weight) for v in (h_outer, h_other)]
+    first += [over_rep(v, early_core) for v in part]
+
+    got0, pieces, came, gain_other, part, names, far0, first = stage(
+        (got0, pieces, came, gain_other, part, names, far0, first)
+    )
+    far1 = lax.ppermute(h_outer[top:], "clus", IN_IN)
+    got1 = inward(pieces[1])
+    other0 = across(got0)
+    order = jnp.arange(every, dtype=jnp.int32)
+    planes = jnp.where(side == 0, jnp.array([1, 0, 2, 3]), jnp.array([2, 3, 1, 0]))
+    ids = (planes[:, None] * rows + order[None, :rows]).reshape(every)
+    before = (names[None, :] < names[:, None]) | (
+        (names[None, :] == names[:, None]) & (ids[None, :] < ids[:, None])
+    )
+    place = jnp.sum(before.astype(jnp.int32), axis=1)
+    at_place = order[:, None] == place[None, :]
+    sorted_labels = jnp.sum(jnp.where(at_place, names[None, :], 0), axis=1)
+    near_side = jnp.where(side == x, mine, came)
+    far_side = jnp.where(side == x, came, mine)
+
+    got1, other0, far0, far1, place, sorted_labels, first, near_side, far_side = stage(
+        (got1, other0, far0, far1, place, sorted_labels, first, near_side, far_side)
+    )
+    far = jnp.concatenate([far0, far1], axis=0)
+    other1 = across(got1)
+    stack = jnp.concatenate([hidden, h_outer, h_other, far], axis=0)
+    late0 = late_part(y, stack, got0, other0)
+    res_near = inward(near_side)
+    res_far = lax.ppermute(far_side, "clus", FAR_IN)
+    res_other = lax.ppermute(after(far_side, late0), "clus", IN_IN)
+    res = jnp.concatenate([near_side, res_near, res_other, res_far], axis=0).astype(F32)
+    first = over_tp(*(jnp.concatenate(v, axis=0) for v in zip(*first)), early_x)
+    last = over_rep(product(after(far, late0), down_weight), early_core)
+    sum0 = over_rep(late0, late_core)
+    late1 = late_part(y, after(stack, *last), got1, other1)
+    last = over_tp(*last, early_x)
+    sum0 = over_tp(*sum0, late_x)
+    sum1 = over_tp(*over_rep(late1, late_core), late_x)
+    early = jnp.concatenate([first, last], axis=0)
+
+    gain_late = jnp.where(x == c, norm_gain, gain_other)
+    gain_early = jnp.where(x == c, gain_other, norm_gain)
+    gain_late = lax.dynamic_slice_in_dim(gain_late, x * half, half, 0)[None, :]
+    gain_early = lax.dynamic_slice_in_dim(gain_early, x * half, half, 0)[None, :]
+    early = ((early + res) * gain_early).astype(BF16)
+    def home(value, near, other, far, where):
+        value = value.reshape(4, rows, half)
+        moved = (
+            lax.ppermute(value[1], ("clus", "rep"), zc(near))
+            + lax.ppermute(value[2], ("clus", "rep"), zc(other))
+            + lax.ppermute(value[3], ("clus", "rep"), zc(far))
+        )
+        return jnp.where(z == where, value[0], moved)
+
+    early_rows = home(
+        early,
+        [((2, 0), (3, 0)), ((1, 1), (0, 1))],
+        [((2, 0), (1, 0)), ((1, 1), (2, 1))],
+        [((2, 0), (0, 0)), ((1, 1), (3, 1))],
+        2 - c,
+    )
+    sum1 = after(sum1, early_rows)
+    late = [
+        ((v + res[:, j * q : k * q]) * gain_late[:, j * q : k * q]).astype(BF16)
+        for v, j, k in ((sum0, 0, 2), (sum1, 2, 4))
+    ]
+    late = jnp.concatenate(late, axis=1)
+
+    tile = 128
+    tiles = every // tile
+    gram, squares = tile_gram(z == 1 + c, place, late, early)
+    gram = gram.reshape(every, 2 * tile)
+    squares = squares.reshape(tiles // 2, 2 * tile)
+    spare = -tiles % 16
+
+    def pack(gram, squares):
+        high = lax.reduce_precision(squares, 8, 7)
+        ends = jnp.zeros((spare, 2 * tile), BF16)
+        return jnp.concatenate(
+            [gram.astype(BF16), high.astype(BF16), (squares - high).astype(BF16), ends], axis=0
+        )
+
+    def meet(gram, squares, met):
+        n = gram.shape[0]
+        ends = met[n : n + tiles].astype(F32)
+        return (
+            gram.astype(F32) + met[:n].astype(F32),
+            squares + ends[: tiles // 2] + ends[tiles // 2 :],
+        )
+
+    for axis, index in (("rep", c), ("tp", x)):
+        n = gram.shape[0] // 2
+        give = lax.dynamic_slice_in_dim(gram, (1 - index) * n, n, 0)
+        keep = lax.dynamic_slice_in_dim(gram, index * n, n, 0)
+        gram, squares = meet(keep, squares, lax.ppermute(pack(give, squares), axis, SWAP))
+    late_rows = home(
+        late,
+        [((1, 0), (0, 0)), ((2, 1), (3, 1))],
+        [((1, 0), (2, 0)), ((2, 1), (1, 1))],
+        [((1, 0), (3, 0)), ((2, 1), (0, 1))],
+        1 + c,
+    )
+    kept = jnp.where(x == c, late_rows, early_rows)
+    came = lax.ppermute(late_rows, ("tp", "rep"), [(2, 0), (1, 3)]) + lax.ppermute(
+        early_rows, ("tp", "rep"), [(0, 2), (3, 1)]
+    )
+    unscaled = jnp.where(
+        x == 0, jnp.concatenate([kept, came], axis=1), jnp.concatenate([came, kept], axis=1)
+    )
+
+    gram = after(gram, late_rows)
+    gram = gram.astype(BF16)
+    gram, squares = meet(gram, squares, lax.ppermute(pack(gram, squares), "clus", IN_IN))
+    gram = gram.reshape(-1, tile, 2 * tile)
+    total = squares.reshape(every)
+
+    n = tiles // 4
+    first = (2 * c + x) * n
+    pad = lambda a, v: jnp.concatenate([a, jnp.full((tile,), v, a.dtype)]).reshape(tiles + 1, tile)
+    span = lambda a: lax.dynamic_slice_in_dim(a, first, n + 1, 0)
+    both = lambda a: jnp.concatenate([a[:-1], a[1:]], axis=1)
+    scale = span(pad(lax.rsqrt(total + EPS), 0.0))
+    tags = span(pad(sorted_labels, -1))
+    sims = gram * scale[:-1, :, None] * both(scale)[:, None, :]
+    at = jnp.arange(tile, dtype=jnp.int32)[:, None] != jnp.arange(2 * tile, dtype=jnp.int32)[None, :]
+    keep = (tags[:-1, :, None] == both(tags)[:, None, :]) & at[None]
+    sims = jnp.where(keep, sims, F32(-4.0))
+    found = jnp.stack([jnp.max(sims, axis=2), jnp.max(sims[:, :, tile:], axis=1)])
+    found = after(found, came)
+    for axis, index in (("tp", x), ("rep", c)):
+        met = lax.ppermute(found, axis, SWAP)
+        found = jnp.where(
+            index == 0, jnp.concatenate([found, met], axis=1), jnp.concatenate([met, found], axis=1)
+        )
+    shifted = jnp.concatenate([jnp.full((1, tile), -4.0, F32), found[1, :-1]], axis=0)
+    best = jnp.maximum(found[0], shifted).reshape(every)
+
+    chosen = place[: 2 * rows, None] == order[None, :]
+    ends = jnp.stack(
+        [
+            jnp.sum(jnp.where(chosen, best[None, :], 0.0), axis=1),
+            jnp.sum(jnp.where(chosen, total[None, :], 0.0), axis=1),
+        ]
+    )
+    ends = jnp.where(inner, ends[:, :rows], lax.ppermute(ends[:, rows:], "clus", IN_OUT))
+    best, total = ends[0], ends[1]
+    score = jnp.where(best > -2.0, D**0.5 * best, F32(-1.0))
+    embedded = (unscaled.astype(F32) * lax.rsqrt(total + EPS)[:, None]).astype(BF16)
+    return (embedded, score)
+
+
 def solution(mesh):
+    size = mesh.shape
+    four = size["clus"] == 4 and size["groups"] == size["tp"] == size["rep"] == 2
     return jax.shard_map(
-        per_device,
+        line_of_four if four else any_mesh,
         mesh=mesh,
         in_specs=(
             P(("groups", "clus"), ("tp", "rep")),

time: 466 us -> 215 us (0.46)
  waiting for transfers between devices: 401 us -> 72.7 us
  starting transfers between devices: 8.07 us -> 67.4 us
  Pallas kernels: 0 us -> 35.8 us
  matrix products: 17 us -> 0 us
  other arithmetic: 5.12 us -> 20.9 us
  blocking collectives: 15.7 us -> 0 us
  between operations: 13.8 us -> 1.91 us
  local copies, waits for them, and re-layouts: 5.35 us -> 15.5 us
    all_gather x1 -> x0, waiting for transfers between devices: 291 us -> none  [per_device(): lax.all_gather(down_weight, 'clus', axis=1, tiled=True)]
    ppermute x0 -> x40, waiting for transfers between devices: none -> 72.7 us  [the longest x3 15.8 us: line_of_four(): lax.ppermute(names, 'clus', pairs)]
    ppermute x0 -> x40, starting transfers between devices: none -> 67.4 us  [the longest x4 21.5 us: inward(): return lax.ppermute(after(value, *gates), 'clus', OUT_IN)]
    all_to_all x2 -> x0, waiting for transfers between devices: 48.1 us -> none  [the longest x1 48 us: per_device(): lax.all_to_all(outgoing, 'clus', split_axis=1, concat_axis=1, tiled=True)]
    pallas_call x0 -> x13, Pallas kernels: none -> 35.8 us  [the longest x4 13.8 us: product(): pl.pallas_call(body, grid=(cols // block,), in_specs=[pl.BlockSpec((m, de...]
    reduce_scatter x1 -> x0, waiting for transfers between devices: 31.2 us -> none  [per_device(): lax.psum_scatter(terms.astype(jnp.bfloat16), ('tp', 'rep'), scatter_dimen...]
    psum x1 -> x0, waiting for transfers between devices: 29.8 us -> none  [per_device(): lax.psum(partial_value.astype(jnp.bfloat16), ('tp', 'rep'))]
    dot_general x3 -> x0, matrix products: 17 us -> none  [the longest x1 11.4 us: per_device(): jnp.dot(hidden, lax.all_gather(down_weight, 'clus', axis=1, tiled=True),...]
  transfers between devices with their start and end apart: 5 -> 40, of which waited for: 4 -> 10; matrix products, arithmetic and copies ran while one was open for 1% -> 12% of each run, Pallas kernels for 0% -> 15%
where the time goes in v1:
time: 215 us; the launch traced here: 214 us
  waiting for transfers between devices  72.7 us (34%)
  starting transfers between devices  67.4 us (31%)
  Pallas kernels  35.8 us (17%)
  other arithmetic  20.9 us (10%)
  local copies, waits for them, and re-layouts  15.5 us (7%)
    ppermute x4, starting transfers between devices, inward(): return lax.ppermute(after(value, *gates), 'clus', OUT_IN)  21.5 us
    ppermute x3, waiting for transfers between devices, line_of_four(): lax.ppermute(names, 'clus', pairs)  15.8 us
    ppermute x2, waiting for transfers between devices, home(): lax.ppermute(value[1], ('clus', 'rep'), zc(near))  13.8 us
    pallas_call x4, Pallas kernels, product(): pl.pallas_call(body, grid=(cols // block,), in_specs=[pl.BlockSpec((m, de...  13.8 us
    pallas_call x2, Pallas kernels, late_part(): pl.pallas_call(body, grid_spec=pltpu.PrefetchScalarGridSpec(num_scalar_pr...  12.4 us
    unnamed x58, local copies, waits for them, and re-layouts  11.3 us
    ppermute x4, waiting for transfers between devices, inward(): return lax.ppermute(after(value, *gates), 'clus', OUT_IN)  11 us
    ppermute x2, waiting for transfers between devices, home(): lax.ppermute(value[3], ('clus', 'rep'), zc(far))  10.3 us
  transfers between devices with their start and end apart: 40, of which 10 were waited for; matrix products, arithmetic and copies ran while one was open for 12% of the time, Pallas kernels for 15%

profile of v1, /device:TPU:0, one launch (start us, length us, event | category | flops | bytes accessed | tf_op | source)
XLA Modules:
  0.0 214.2 jit_solution(8056022669406450769)
XLA Ops:
  0.6 5.0 %collective-permute-start = (bf16[384,2048]{1,0:T(8,128)(2,1)}, bf16[384,2048]{1,0:T(8,128)(2,1)S(1)}, u32[]{:S(2)}, u32[]{:S(2)}) collective-permute-start(bf16[384,2048]{1,0:T(8,128)(2,1)} %a.1), channel_id=1, source_target_pairs={{0,4},{12,8},{1,5},{13,9},{2,6},{14,10},{3,7},{15,11},{16,20},{28,... | collective-permute-start | bytes 4718600 | tf_op jit(solution)/shard_map/ppermute | solution.py:251
  5.7 1.9 collective-permute-start.1
  8.2 2.8 %collective-permute-start.2 = (s32[384]{0:T(512)S(1)}, s32[384]{0:T(512)S(1)}, u32[]{:S(2)}, u32[]{:S(2)}) collective-permute-start(s32[384]{0:T(512)S(1)} %reduce.1), channel_id=1, source_target_pairs={{0,4},{12,8},{1,5},{13,9},{2,6},{14,10},{3,7},{15,11},{16,20},{28,... | collective-permute-start | bytes 4616 | tf_op jit(solution)/shard_map/ppermute | solution.py:258
  11.7 4.0 %collective-permute-start.4 = (s32[384]{0:T(512)S(1)}, s32[384]{0:T(512)S(1)}, u32[]{:S(2)}, u32[]{:S(2)}) collective-permute-start(s32[384]{0:T(512)S(1)} %reduce.1), channel_id=1, source_target_pairs={{0,8},{12,4},{1,9},{13,5},{2,10},{14,6},{3,11},{15,7},{16,24},{28,... | collective-permute-start | bytes 4616 | tf_op jit(solution)/shard_map/ppermute | solution.py:258
  15.8 1.8 fusion.29
  17.6 1.5 pad_maximum_fusion.3
  19.2 1.6 copy-done.2
  20.9 3.0 %product.4.a.c = bf16[384,1024]{1,0:T(8,128)(2,1)S(1)} custom-call(bf16[384,2048]{1,0:T(8,128)(2,1)S(1)} %copy-done.4, bf16[2048,1024]{1,0:T(8,128)(2,1)S(1)} %copy-done.2), custom_call_target="tpu_custom_call" | custom-call | flops 1024 | bytes 1024 | tf_op jit(solution)/shard_map/product/pallas_call | solution.py:127
  23.8 15.7 %collective-permute-done.2 = s32[384]{0:T(512)S(1)} collective-permute-done((s32[384]{0:T(512)S(1)}, s32[384]{0:T(512)S(1)}, u32[]{:S(2)}, u32[]{:S(2)}) %collective-permute-start.2) | collective-permute-done | bytes 1568 | tf_op jit(solution)/shard_map/ppermute | solution.py:258
  40.2 1.5 collective-permute-start.6
  41.7 1.5 collective-permute-start.9
  43.2 7.3 %collective-permute-start.5 = (bf16[1024,512]{1,0:T(8,128)(2,1)}, bf16[1024,512]{1,0:T(8,128)(2,1)}, u32[]{:S(2)}, u32[]{:S(2)}) collective-permute-start(bf16[1024,512]{1,0:T(8,128)(2,1)} %get-tuple-element.59), channel_id=1, source_target_pairs={{0,4},{12,8},{1,5},{13,9},{2,6},{14,10},{3,7},{15,11},{16,20},{28,... | collective-permute-start | bytes 3145736 | tf_op jit(solution)/shard_map/ppermute | solution.py:251
  51.8 1.5 collective-permute-start.8
  53.3 4.9 %product.6.a.c = bf16[384,1024]{1,0:T(8,128)(2,1)} custom-call(bf16[384,2048]{1,0:T(8,128)(2,1)} %collective-permute-done.1.a, bf16[2048,1024]{1,0:T(8,128)(2,1)S(1)} %copy-done.2), custom_call_target="tpu_custom_call" | custom-call | flops 1024 | bytes 1024 | tf_op jit(solution)/shard_map/product/pallas_call | solution.py:127
  58.2 1.5 collective-permute-start.11
  59.7 3.0 %product.5.a.c = bf16[384,1024]{1,0:T(8,128)(2,1)S(1)} custom-call(bf16[384,2048]{1,0:T(8,128)(2,1)S(1)} %collective-permute-done.a, bf16[2048,1024]{1,0:T(8,128)(2,1)S(1)} %copy-done.2), custom_call_target="tpu_custom_call" | custom-call | flops 1024 | bytes 1024 | tf_op jit(solution)/shard_map/product/pallas_call | solution.py:127
  62.7 1.6 collective-permute-start.10
  64.4 1.6 constant_dynamic-update-slice_fusion.4
  66.7 1.3 fold.6
  68.9 1.5 fold.8
  71.4 1.4 fold.7
  72.9 6.1 %collective-permute-start.12 = (bf16[1024,512]{1,0:T(8,128)(2,1)S(1)}, bf16[1024,512]{1,0:T(8,128)(2,1)}, u32[]{:S(2)}, u32[]{:S(2)}) collective-permute-start(bf16[1024,512]{1,0:T(8,128)(2,1)S(1)} %copy-done.11), channel_id=1, source_target_pairs={{0,4},{12,8},{1,5},{13,9},{2,6},{14,10},{3,7},{15,11},{16,20},{28,... | collective-permute-start | bytes 3145736 | tf_op jit(solution)/shard_map/ppermute | solution.py:251
  78.9 1.5 collective-permute-start.13
  80.5 1.6 constant_dynamic-update-slice_fusion.2
  83.7 3.0 %convert_reduce_fusion = s32[1536]{0:T(1024)S(1)} fusion(s32[1536]{0:T(1024)S(1)} %add.151, s32[1536]{0:T(1024)S(1)} %copy-done.20), kind=kLoop, calls=%fused_computation.2 | loop fusion | flops 16513536 | bytes 18432 | tf_op jit(solution)/shard_map/reduce_sum | solution.py:291
  86.7 1.6 select_reduce_fusion
  88.3 9.5 %collective-permute-done.12.own = bf16[1024,512]{1,0:T(8,128)(2,1)} collective-permute-done((bf16[1024,512]{1,0:T(8,128)(2,1)S(1)}, bf16[1024,512]{1,0:T(8,128)(2,1)}, u32[]{:S(2)}, u32[]{:S(2)}) %collective-permute-start.12) | collective-permute-done | bytes 1048608 | tf_op jit(solution)/shard_map/ppermute | solution.py:251
  97.9 4.4 %collective-permute-done.13.other = bf16[1024,512]{1,0:T(8,128)(2,1)S(1)} collective-permute-done((bf16[1024,512]{1,0:T(8,128)(2,1)}, bf16[1024,512]{1,0:T(8,128)(2,1)S(1)}, u32[]{:S(2)}, u32[]{:S(2)}) %collective-permute-start.13) | collective-permute-done | bytes 1048608 | tf_op jit(solution)/shard_map/ppermute | solution.py:248
  102.3 1.5 collective-permute-start.21
  105.0 1.7 collective-permute-start.24
  108.0 6.9 %late_part.2.a.c = bf16[1536,512]{1,0:T(8,128)(2,1)S(1)} custom-call(s32[1]{0:T(128)} %bitcast.1._, bf16[1536,2048]{1,0:T(8,128)(2,1)S(1)} %constant_dynamic-update-slice_fusion.a.b, bf16[1536,2048]{1,0:T(8,128)(2,1)S(1)} %constant_dynamic-update-slice_fusion.a.b, bf16[1024,512]{1,0:T(8,128)(2,1)} %collective-permute-done.5.own, ...), custom_call_target="tpu_custom_call" | custom-call | flops 1024 | bytes 1024 | tf_op jit(solution)/shard_map/late_part/pallas_call | solution.py:99
  114.9 1.3 pad_maximum_fusion.1.a
  116.3 3.0 %product.7.a.c = bf16[384,1024]{1,0:T(8,128)(2,1)S(1)} custom-call(bf16[384,2048]{1,0:T(8,128)(2,1)S(1)} %pad_maximum_fusion.1.a, bf16[2048,1024]{1,0:T(8,128)(2,1)S(1)} %copy-done.3), custom_call_target="tpu_custom_call" | custom-call | flops 1024 | bytes 1024 | tf_op jit(solution)/shard_map/product/pallas_call | solution.py:127
  120.2 3.2 %collective-permute-start.19 = (bf16[384,512]{1,0:T(8,128)(2,1)}, bf16[384,512]{1,0:T(8,128)(2,1)S(1)}, u32[]{:S(2)}, u32[]{:S(2)}) collective-permute-start(bf16[384,512]{1,0:T(8,128)(2,1)} %get-tuple-element.90), channel_id=1, source_target_pairs={{0,8},{12,4},{1,9},{13,5},{2,10},{14,6},{3,11},{15,7},{16,24},{28,... | collective-permute-start | bytes 1179656 | tf_op jit(solution)/shard_map/ppermute | solution.py:305
  124.1 3.1 %collective-permute-start.17 = (bf16[384,512]{1,0:T(8,128)(2,1)S(1)}, bf16[384,512]{1,0:T(8,128)(2,1)S(1)}, u32[]{:S(2)}, u32[]{:S(2)}) collective-permute-start(bf16[384,512]{1,0:T(8,128)(2,1)S(1)} %get-tuple-element.88), channel_id=1, source_target_pairs={{0,4},{12,8},{1,5},{13,9},{2,6},{14,10},{3,7},{15,11},{16,20},{28,... | collective-permute-start | bytes 1179656 | tf_op jit(solution)/shard_map/ppermute | solution.py:251
  128.1 2.8 %copy-done.1 = bf16[1536,2048]{1,0:T(8,128)(2,1)S(1)} copy-done((bf16[1536,2048]{1,0:T(8,128)(2,1)S(1)}, bf16[1536,2048]{1,0:T(8,128)(2,1)}, u32[]{:S(2)}) %copy-start.1) | copy-done | bytes 6291480
  130.8 5.5 %late_part.3.a.c = bf16[1536,512]{1,0:T(8,128)(2,1)S(1)} custom-call(s32[1]{0:T(128)} %bitcast.1._, bf16[1536,2048]{1,0:T(8,128)(2,1)S(1)} %copy-done.1, bf16[1536,2048]{1,0:T(8,128)(2,1)S(1)} %copy-done.1, bf16[1024,512]{1,0:T(8,128)(2,1)} %collective-permute-done.12.own, bf16[1024,512]{1,0:T(8,128)(2,1)} %collective-permute-done.21.other), custom_call_target="tpu_custom_call" | custom-call | flops 1024 | bytes 1024 | tf_op jit(solution)/shard_map/late_part/pallas_call | solution.py:99
  137.2 1.6 maximum_add_fusion.1
  139.9 1.4 collective-permute-done.17
  148.3 10.3 %collective-permute-done.28 = bf16[384,512]{1,0:T(8,128)(2,1)S(1)} collective-permute-done((bf16[384,512]{1,0:T(8,128)(2,1)S(1)}, bf16[384,512]{1,0:T(8,128)(2,1)S(1)}, u32[]{:S(2)}, u32[]{:S(2)}) %collective-permute-start.28) | collective-permute-done | bytes 393248 | tf_op jit(solution)/shard_map/ppermute | solution.py:327
  159.6 3.6 %tile_gram.1 = (bf16[12,128,256]{2,1,0:T(8,128)(2,1)S(1)}, f32[12,128]{1,0:T(8,128)S(1)}) custom-call(s32[1]{0:T(128)} %bitcast.9.flag, s32[1,1536]{1,0:T(1,128)S(1)} %reshape.142.place, bf16[1536,512]{1,0:T(8,128)(2,1)S(1)} %pad_maximum_fusion.late, bf16[1536,512]{1,0:T(8,128)(2,1)S(1)} %fusion.1.early), custom_call_target="tpu_custom_call" | custom-call | flops 1024 | bytes 1024 | tf_op jit(solution)/shard_map/tile_gram/pallas_call | solution.py:200
  164.7 2.7 %collective-permute-start.33 = (bf16[384,512]{1,0:T(8,128)(2,1)S(1)}, bf16[384,512]{1,0:T(8,128)(2,1)S(1)}, u32[]{:S(2)}, u32[]{:S(2)}) collective-permute-start(bf16[384,512]{1,0:T(8,128)(2,1)S(1)} %slice_select_fusion), channel_id=1, source_target_pairs={{0,2},{3,1},{4,6},{7,5},{8,10},{11,9},{12,14},{15,13},{16,18},{19,... | collective-permute-start | bytes 1179656 | tf_op jit(solution)/shard_map/ppermute | solution.py:380
  172.1 13.8 %collective-permute-done.29 = bf16[384,512]{1,0:T(8,128)(2,1)S(1)} collective-permute-done((bf16[384,512]{1,0:T(8,128)(2,1)S(1)}, bf16[384,512]{1,0:T(8,128)(2,1)S(1)}, u32[]{:S(2)}, u32[]{:S(2)}) %collective-permute-start.29) | collective-permute-done | bytes 393248 | tf_op jit(solution)/shard_map/ppermute | solution.py:325
  188.5 7.5 %collective-permute-done.32 = bf16[384,512]{1,0:T(8,128)(2,1)S(1)} collective-permute-done((bf16[384,512]{1,0:T(8,128)(2,1)S(1)}, bf16[384,512]{1,0:T(8,128)(2,1)S(1)}, u32[]{:S(2)}, u32[]{:S(2)}) %collective-permute-start.32) | collective-permute-done | bytes 393248 | tf_op jit(solution)/shard_map/ppermute | solution.py:380
  196.8 3.6 %collective-permute-done.37 = f32[2,3,128]{2,1,0:T(4,128)S(1)} collective-permute-done((f32[2,3,128]{2,1,0:T(4,128)S(1)}, f32[2,3,128]{2,1,0:T(4,128)S(1)}, u32[]{:S(2)}, u32[]{:S(2)}) %collective-permute-start.37) | collective-permute-done | bytes 3104 | tf_op jit(solution)/shard_map/ppermute | solution.py:407
  200.3 2.9 %collective-permute-start.38 = (f32[2,6,128]{2,1,0:T(8,128)S(1)}, f32[2,6,128]{2,1,0:T(8,128)S(1)}, u32[]{:S(2)}, u32[]{:S(2)}) collective-permute-start(f32[2,6,128]{2,1,0:T(8,128)S(1)} %maximum_select_fusion.2), channel_id=1, source_target_pairs={{0,1},{1,0},{2,3},{3,2},{4,5},{5,4},{6,7},{7,6},{8,9},{9,8},{10,11... | collective-permute-start | bytes 18440 | tf_op jit(solution)/shard_map/ppermute | solution.py:407
  204.1 1.6 select_reduce_fusion.2
  207.1 5.4 %collective-permute-done.39 = f32[2,384]{1,0:T(2,128)S(1)} collective-permute-done((f32[2,384]{1,0:T(2,128)S(1)}, f32[2,384]{1,0:T(2,128)S(1)}, u32[]{:S(2)}, u32[]{:S(2)}) %collective-permute-start.39) | collective-permute-done | bytes 3104 | tf_op jit(solution)/shard_map/ppermute | solution.py:421
  (185 shorter events, 35.0 us)
Async XLA Ops:
  0.6 39.5 %collective-permute-start = (bf16[384,2048]{1,0:T(8,128)(2,1)}, bf16[384,2048]{1,0:T(8,128)(2,1)S(1)}, u32[]{:S(2)}, u32[]{:S(2)}) collective-permute-start(bf16[384,2048]{1,0:T(8,128)(2,1)} %a.1), channel_id=1, source_target_pairs={{0,4},{12,8},{1,5},{13,9},{2,6},{14,10},{3,7},{15,11},{16,20},{28,... | collective-permute-start | bytes 4718600 | tf_op jit(solution)/shard_map/ppermute | solution.py:251
  5.7 34.5 %collective-permute-start.1 = (bf16[384,2048]{1,0:T(8,128)(2,1)}, bf16[384,2048]{1,0:T(8,128)(2,1)}, u32[]{:S(2)}, u32[]{:S(2)}) collective-permute-start(bf16[384,2048]{1,0:T(8,128)(2,1)} %a.1), channel_id=1, source_target_pairs={{4,8},{8,4},{5,9},{9,5},{6,10},{10,6},{7,11},{11,7},{20,24},{24,20... | collective-permute-start | bytes 4718600 | tf_op jit(solution)/shard_map/ppermute | solution.py:256
  8.2 31.3 %collective-permute-start.2 = (s32[384]{0:T(512)S(1)}, s32[384]{0:T(512)S(1)}, u32[]{:S(2)}, u32[]{:S(2)}) collective-permute-start(s32[384]{0:T(512)S(1)} %reduce.1), channel_id=1, source_target_pairs={{0,4},{12,8},{1,5},{13,9},{2,6},{14,10},{3,7},{15,11},{16,20},{28,... | collective-permute-start | bytes 4616 | tf_op jit(solution)/shard_map/ppermute | solution.py:258
  11.1 28.5 %collective-permute-start.3 = (s32[384]{0:T(512)S(1)}, s32[384]{0:T(512)S(1)}, u32[]{:S(2)}, u32[]{:S(2)}) collective-permute-start(s32[384]{0:T(512)S(1)} %reduce.1), channel_id=1, source_target_pairs={{4,8},{8,4},{5,9},{9,5},{6,10},{10,6},{7,11},{11,7},{20,24},{24,20... | collective-permute-start | bytes 4616 | tf_op jit(solution)/shard_map/ppermute | solution.py:258
  11.7 27.8 %collective-permute-start.4 = (s32[384]{0:T(512)S(1)}, s32[384]{0:T(512)S(1)}, u32[]{:S(2)}, u32[]{:S(2)}) collective-permute-start(s32[384]{0:T(512)S(1)} %reduce.1), channel_id=1, source_target_pairs={{0,8},{12,4},{1,9},{13,5},{2,10},{14,6},{3,11},{15,7},{16,24},{28,... | collective-permute-start | bytes 4616 | tf_op jit(solution)/shard_map/ppermute | solution.py:258
  40.2 13.1 %collective-permute-start.6 = (bf16[384,512]{1,0:T(8,128)(2,1)S(1)}, bf16[384,512]{1,0:T(8,128)(2,1)S(1)}, u32[]{:S(2)}, u32[]{:S(2)}) collective-permute-start(bf16[384,512]{1,0:T(8,128)(2,1)S(1)} %constant_dynamic-slice_fusion.4), channel_id=1, source_target_pairs={{0,2},{2,0},{1,3},{3,1},{4,6},{6,4},{5,7},{7,5},{8,10},{10,8},{9,1... | collective-permute-start | bytes 1179656 | tf_op jit(solution)/shard_map/ppermute | solution.py:273
  41.7 24.3 %collective-permute-start.9 = (bf16[384,1024]{1,0:T(8,128)(2,1)S(1)}, bf16[384,1024]{1,0:T(8,128)(2,1)}, u32[]{:S(2)}, u32[]{:S(2)}) collective-permute-start(bf16[384,1024]{1,0:T(8,128)(2,1)S(1)} %product.4.a.c), channel_id=1, source_target_pairs={{4,5},{9,8},{6,7},{11,10},{20,21},{25,24},{22,23},{27,26}} | collective-permute-start | bytes 2359304 | tf_op jit(solution)/shard_map/ppermute | solution.py:242
  43.2 29.6 %collective-permute-start.5 = (bf16[1024,512]{1,0:T(8,128)(2,1)}, bf16[1024,512]{1,0:T(8,128)(2,1)}, u32[]{:S(2)}, u32[]{:S(2)}) collective-permute-start(bf16[1024,512]{1,0:T(8,128)(2,1)} %get-tuple-element.59), channel_id=1, source_target_pairs={{0,4},{12,8},{1,5},{13,9},{2,6},{14,10},{3,7},{15,11},{16,20},{28,... | collective-permute-start | bytes 3145736 | tf_op jit(solution)/shard_map/ppermute | solution.py:251
  51.8 21.1 %collective-permute-start.8 = (bf16[192,2048]{1,0:T(8,128)(2,1)}, bf16[192,2048]{1,0:T(8,128)(2,1)}, u32[]{:S(2)}, u32[]{:S(2)}) collective-permute-start(bf16[192,2048]{1,0:T(8,128)(2,1)} %get-tuple-element.135), channel_id=1, source_target_pairs={{4,8},{8,4},{5,9},{9,5},{6,10},{10,6},{7,11},{11,7},{20,24},{24,20... | collective-permute-start | bytes 2359304 | tf_op jit(solution)/shard_map/ppermute | solution.py:272
  58.2 10.7 %collective-permute-start.11 = (bf16[384,1024]{1,0:T(8,128)(2,1)}, bf16[384,1024]{1,0:T(8,128)(2,1)}, u32[]{:S(2)}, u32[]{:S(2)}) collective-permute-start(bf16[384,1024]{1,0:T(8,128)(2,1)} %product.6.a.c), channel_id=1, source_target_pairs={{4,5},{9,8},{6,7},{11,10},{20,21},{25,24},{22,23},{27,26}} | collective-permute-start | bytes 2359304 | tf_op jit(solution)/shard_map/ppermute | solution.py:242
  62.7 8.7 %collective-permute-start.10 = (bf16[384,1024]{1,0:T(8,128)(2,1)S(1)}, bf16[384,1024]{1,0:T(8,128)(2,1)}, u32[]{:S(2)}, u32[]{:S(2)}) collective-permute-start(bf16[384,1024]{1,0:T(8,128)(2,1)S(1)} %product.5.a.c), channel_id=1, source_target_pairs={{4,5},{9,8},{6,7},{11,10},{20,21},{25,24},{22,23},{27,26}} | collective-permute-start | bytes 2359304 | tf_op jit(solution)/shard_map/ppermute | solution.py:242
  66.0 6.8 %collective-permute-start.7 = (f32[1024]{0:T(1024)S(1)}, f32[1024]{0:T(1024)S(1)}, u32[]{:S(2)}, u32[]{:S(2)}) collective-permute-start(f32[1024]{0:T(1024)S(1)} %copy-done.21), channel_id=1, source_target_pairs={{0,2},{2,0},{1,3},{3,1},{4,6},{6,4},{5,7},{7,5},{8,10},{10,8},{9,1... | collective-permute-start | bytes 12296 | tf_op jit(solution)/shard_map/ppermute | solution.py:274
  72.8 10.9 %copy-start.9 = (f32[384,512]{1,0:T(8,128)}, f32[384,512]{1,0:T(8,128)S(1)}, u32[]{:S(2)}) copy-start(f32[384,512]{1,0:T(8,128)S(1)} %get-tuple-element.100) | copy-start | bytes 2359300
  72.8 10.0 %copy-start.13 = (bf16[384,1024]{1,0:T(8,128)(2,1)S(1)}, bf16[384,1024]{1,0:T(8,128)(2,1)}, u32[]{:S(2)}) copy-start(bf16[384,1024]{1,0:T(8,128)(2,1)} %param.8) | copy-start | bytes 2359300
  72.8 10.0 %copy-start.23 = (f32[1024]{0:T(1024)}, f32[1024]{0:T(1024)S(1)}, u32[]{:S(2)}) copy-start(f32[1024]{0:T(1024)S(1)} %collective-permute-done.7) | copy-start | bytes 12292
  72.9 10.8 %copy-start.20 = (s32[1536]{0:T(1024)S(1)}, s32[1536]{0:T(1024)}, u32[]{:S(2)}) copy-start(s32[1536]{0:T(1024)} %pad_add_fusion) | copy-start | bytes 18436
  72.9 25.0 %collective-permute-start.12 = (bf16[1024,512]{1,0:T(8,128)(2,1)S(1)}, bf16[1024,512]{1,0:T(8,128)(2,1)}, u32[]{:S(2)}, u32[]{:S(2)}) collective-permute-start(bf16[1024,512]{1,0:T(8,128)(2,1)S(1)} %copy-done.11), channel_id=1, source_target_pairs={{0,4},{12,8},{1,5},{13,9},{2,6},{14,10},{3,7},{15,11},{16,20},{28,... | collective-permute-start | bytes 3145736 | tf_op jit(solution)/shard_map/ppermute | solution.py:251
  78.9 23.3 %collective-permute-start.13 = (bf16[1024,512]{1,0:T(8,128)(2,1)}, bf16[1024,512]{1,0:T(8,128)(2,1)S(1)}, u32[]{:S(2)}, u32[]{:S(2)}) collective-permute-start(bf16[1024,512]{1,0:T(8,128)(2,1)} %collective-permute-done.5.own), channel_id=1, source_target_pairs={{0,16},{16,0},{1,17},{17,1},{2,18},{18,2},{3,19},{19,3},{4,20},{20... | collective-permute-start | bytes 3145736 | tf_op jit(solution)/shard_map/ppermute | solution.py:248
  82.1 6.3 %collective-permute-start.14 = (bf16[192,2048]{1,0:T(8,128)(2,1)S(1)}, bf16[192,2048]{1,0:T(8,128)(2,1)S(1)}, u32[]{:S(2)}, u32[]{:S(2)}) collective-permute-start(bf16[192,2048]{1,0:T(8,128)(2,1)S(1)} %copy-done.14), channel_id=1, source_target_pairs={{4,8},{8,4},{5,9},{9,5},{6,10},{10,6},{7,11},{11,7},{20,24},{24,20... | collective-permute-start | bytes 2359304 | tf_op jit(solution)/shard_map/ppermute | solution.py:282
  86.7 59.5 %copy-start.19 = (s32[1536]{0:T(1024)}, s32[1536]{0:T(1024)S(1)}, u32[]{:S(2)}) copy-start(s32[1536]{0:T(1024)S(1)} %convert_reduce_fusion) | copy-start | bytes 18436
  102.3 25.1 %collective-permute-start.21 = (bf16[1024,512]{1,0:T(8,128)(2,1)}, bf16[1024,512]{1,0:T(8,128)(2,1)}, u32[]{:S(2)}, u32[]{:S(2)}) collective-permute-start(bf16[1024,512]{1,0:T(8,128)(2,1)} %collective-permute-done.12.own), channel_id=1, source_target_pairs={{0,16},{16,0},{1,17},{17,1},{2,18},{18,2},{3,19},{19,3},{4,20},{20... | collective-permute-start | bytes 3145736 | tf_op jit(solution)/shard_map/ppermute | solution.py:248
  105.0 31.4 %collective-permute-start.24 = (bf16[1152,512]{1,0:T(8,128)(2,1)}, bf16[1152,512]{1,0:T(8,128)(2,1)}, u32[]{:S(2)}, u32[]{:S(2)}) collective-permute-start(bf16[1152,512]{1,0:T(8,128)(2,1)} %pad_maximum_fusion.2), channel_id=1, source_target_pairs={{5,7},{7,5},{8,10},{10,8},{21,23},{23,21},{24,26},{26,24}} | collective-permute-start | bytes 3538952 | tf_op jit(solution)/shard_map/ppermute | solution.py:245
  119.3 4.8 %collective-permute-start.20 = (bf16[384,1024]{1,0:T(8,128)(2,1)S(1)}, bf16[384,1024]{1,0:T(8,128)(2,1)S(1)}, u32[]{:S(2)}, u32[]{:S(2)}) collective-permute-start(bf16[384,1024]{1,0:T(8,128)(2,1)S(1)} %product.7.a.c), channel_id=1, source_target_pairs={{4,5},{9,8},{6,7},{11,10},{20,21},{25,24},{22,23},{27,26}} | collective-permute-start | bytes 2359304 | tf_op jit(solution)/shard_map/ppermute | solution.py:242
  120.2 21.1 %collective-permute-start.19 = (bf16[384,512]{1,0:T(8,128)(2,1)}, bf16[384,512]{1,0:T(8,128)(2,1)S(1)}, u32[]{:S(2)}, u32[]{:S(2)}) collective-permute-start(bf16[384,512]{1,0:T(8,128)(2,1)} %get-tuple-element.90), channel_id=1, source_target_pairs={{0,8},{12,4},{1,9},{13,5},{2,10},{14,6},{3,11},{15,7},{16,24},{28,... | collective-permute-start | bytes 1179656 | tf_op jit(solution)/shard_map/ppermute | solution.py:305
  123.4 16.5 %collective-permute-start.18 = (bf16[384,512]{1,0:T(8,128)(2,1)}, bf16[384,512]{1,0:T(8,128)(2,1)S(1)}, u32[]{:S(2)}, u32[]{:S(2)}) collective-permute-start(bf16[384,512]{1,0:T(8,128)(2,1)} %get-tuple-element.90), channel_id=1, source_target_pairs={{4,8},{8,4},{5,9},{9,5},{6,10},{10,6},{7,11},{11,7},{20,24},{24,20... | collective-permute-start | bytes 1179656 | tf_op jit(solution)/shard_map/ppermute | solution.py:306
  124.1 17.2 %collective-permute-start.17 = (bf16[384,512]{1,0:T(8,128)(2,1)S(1)}, bf16[384,512]{1,0:T(8,128)(2,1)S(1)}, u32[]{:S(2)}, u32[]{:S(2)}) collective-permute-start(bf16[384,512]{1,0:T(8,128)(2,1)S(1)} %get-tuple-element.88), channel_id=1, source_target_pairs={{0,4},{12,8},{1,5},{13,9},{2,6},{14,10},{3,7},{15,11},{16,20},{28,... | collective-permute-start | bytes 1179656 | tf_op jit(solution)/shard_map/ppermute | solution.py:251
  127.4 11.4 %collective-permute-start.25 = (bf16[384,512]{1,0:T(8,128)(2,1)S(1)}, bf16[384,512]{1,0:T(8,128)(2,1)S(1)}, u32[]{:S(2)}, u32[]{:S(2)}) collective-permute-start(bf16[384,512]{1,0:T(8,128)(2,1)S(1)} %get-tuple-element.94), channel_id=1, source_target_pairs={{5,7},{7,5},{8,10},{10,8},{21,23},{23,21},{24,26},{26,24}} | collective-permute-start | bytes 1179656 | tf_op jit(solution)/shard_map/ppermute | solution.py:245
  136.4 8.4 %collective-permute-start.22 = (bf16[1536,512]{1,0:T(8,128)(2,1)S(1)}, bf16[1536,512]{1,0:T(8,128)(2,1)S(1)}, u32[]{:S(2)}, u32[]{:S(2)}) collective-permute-start(bf16[1536,512]{1,0:T(8,128)(2,1)S(1)} %late_part.3.a.c), channel_id=1, source_target_pairs={{5,4},{8,9},{7,6},{10,11},{21,20},{24,25},{23,22},{26,27}} | collective-permute-start | bytes 4718600 | tf_op jit(solution)/shard_map/ppermute | solution.py:242
  138.8 7.9 %collective-permute-start.15 = (bf16[1536,512]{1,0:T(8,128)(2,1)S(1)}, bf16[1536,512]{1,0:T(8,128)(2,1)S(1)}, u32[]{:S(2)}, u32[]{:S(2)}) collective-permute-start(bf16[1536,512]{1,0:T(8,128)(2,1)S(1)} %late_part.2.a.c), channel_id=1, source_target_pairs={{5,4},{8,9},{7,6},{10,11},{21,20},{24,25},{23,22},{26,27}} | collective-permute-start | bytes 4718600 | tf_op jit(solution)/shard_map/ppermute | solution.py:242
  142.1 6.2 %collective-permute-start.26 = (bf16[384,512]{1,0:T(8,128)(2,1)S(1)}, bf16[384,512]{1,0:T(8,128)(2,1)S(1)}, u32[]{:S(2)}, u32[]{:S(2)}) collective-permute-start(bf16[384,512]{1,0:T(8,128)(2,1)S(1)} %get-tuple-element.133), channel_id=1, source_target_pairs={{8,12},{5,1},{10,14},{7,3},{24,28},{21,17},{26,30},{23,19}} | collective-permute-start | bytes 1179656 | tf_op jit(solution)/shard_map/ppermute | solution.py:325
  142.8 5.5 %collective-permute-start.27 = (bf16[384,512]{1,0:T(8,128)(2,1)S(1)}, bf16[384,512]{1,0:T(8,128)(2,1)S(1)}, u32[]{:S(2)}, u32[]{:S(2)}) collective-permute-start(bf16[384,512]{1,0:T(8,128)(2,1)S(1)} %get-tuple-element.131), channel_id=1, source_target_pairs={{8,4},{5,9},{10,6},{7,11},{24,20},{21,25},{26,22},{23,27}} | collective-permute-start | bytes 1179656 | tf_op jit(solution)/shard_map/ppermute | solution.py:326
  143.5 15.1 %collective-permute-start.28 = (bf16[384,512]{1,0:T(8,128)(2,1)S(1)}, bf16[384,512]{1,0:T(8,128)(2,1)S(1)}, u32[]{:S(2)}, u32[]{:S(2)}) collective-permute-start(bf16[384,512]{1,0:T(8,128)(2,1)S(1)} %get-tuple-element.132), channel_id=1, source_target_pairs={{8,0},{5,13},{10,2},{7,15},{24,16},{21,29},{26,18},{23,31}} | collective-permute-start | bytes 1179656 | tf_op jit(solution)/shard_map/ppermute | solution.py:327
  145.5 13.1 %collective-permute-start.23 = (bf16[1536,256]{1,0:T(8,128)(2,1)S(1)}, bf16[1536,256]{1,0:T(8,128)(2,1)S(1)}, u32[]{:S(2)}, u32[]{:S(2)}) collective-permute-start(bf16[1536,256]{1,0:T(8,128)(2,1)S(1)} %get-tuple-element.98), channel_id=1, source_target_pairs={{4,6},{6,4},{9,11},{11,9},{20,22},{22,20},{25,27},{27,25}} | collective-permute-start | bytes 2359304 | tf_op jit(solution)/shard_map/ppermute | solution.py:245
  147.5 11.3 %collective-permute-start.16 = (bf16[1536,256]{1,0:T(8,128)(2,1)S(1)}, bf16[1536,256]{1,0:T(8,128)(2,1)S(1)}, u32[]{:S(2)}, u32[]{:S(2)}) collective-permute-start(bf16[1536,256]{1,0:T(8,128)(2,1)S(1)} %get-tuple-element.87), channel_id=1, source_target_pairs={{4,6},{6,4},{9,11},{11,9},{20,22},{22,20},{25,27},{27,25}} | collective-permute-start | bytes 2359304 | tf_op jit(solution)/shard_map/ppermute | solution.py:245
  163.4 6.8 %collective-permute-start.34 = (bf16[784,256]{1,0:T(8,128)(2,1)S(1)}, bf16[784,256]{1,0:T(8,128)(2,1)}, u32[]{:S(2)}, u32[]{:S(2)}) collective-permute-start(bf16[784,256]{1,0:T(8,128)(2,1)S(1)} %pad_maximum_fusion.5), channel_id=1, source_target_pairs={{0,1},{1,0},{2,3},{3,2},{4,5},{5,4},{6,7},{7,6},{8,9},{9,8},{10,11... | collective-permute-start | bytes 1204232 | tf_op jit(solution)/shard_map/ppermute | solution.py:371
  164.7 23.8 %collective-permute-start.33 = (bf16[384,512]{1,0:T(8,128)(2,1)S(1)}, bf16[384,512]{1,0:T(8,128)(2,1)S(1)}, u32[]{:S(2)}, u32[]{:S(2)}) collective-permute-start(bf16[384,512]{1,0:T(8,128)(2,1)S(1)} %slice_select_fusion), channel_id=1, source_target_pairs={{0,2},{3,1},{4,6},{7,5},{8,10},{11,9},{12,14},{15,13},{16,18},{19,... | collective-permute-start | bytes 1179656 | tf_op jit(solution)/shard_map/ppermute | solution.py:380
  167.5 18.5 %collective-permute-start.29 = (bf16[384,512]{1,0:T(8,128)(2,1)S(1)}, bf16[384,512]{1,0:T(8,128)(2,1)S(1)}, u32[]{:S(2)}, u32[]{:S(2)}) collective-permute-start(bf16[384,512]{1,0:T(8,128)(2,1)S(1)} %get-tuple-element.129), channel_id=1, source_target_pairs={{4,0},{9,13},{6,2},{11,15},{20,16},{25,29},{22,18},{27,31}} | collective-permute-start | bytes 1179656 | tf_op jit(solution)/shard_map/ppermute | solution.py:325
  168.8 17.2 %collective-permute-start.30 = (bf16[384,512]{1,0:T(8,128)(2,1)S(1)}, bf16[384,512]{1,0:T(8,128)(2,1)S(1)}, u32[]{:S(2)}, u32[]{:S(2)}) collective-permute-start(bf16[384,512]{1,0:T(8,128)(2,1)S(1)} %get-tuple-element.128), channel_id=1, source_target_pairs={{4,8},{9,5},{6,10},{11,7},{20,24},{25,21},{22,26},{27,23}} | collective-permute-start | bytes 1179656 | tf_op jit(solution)/shard_map/ppermute | solution.py:326
  169.5 16.5 %collective-permute-start.31 = (bf16[384,512]{1,0:T(8,128)(2,1)S(1)}, bf16[384,512]{1,0:T(8,128)(2,1)S(1)}, u32[]{:S(2)}, u32[]{:S(2)}) collective-permute-start(bf16[384,512]{1,0:T(8,128)(2,1)S(1)} %get-tuple-element.130), channel_id=1, source_target_pairs={{4,12},{9,1},{6,14},{11,3},{20,28},{25,17},{22,30},{27,19}} | collective-permute-start | bytes 1179656 | tf_op jit(solution)/shard_map/ppermute | solution.py:327
  172.0 24.1 %copy-start.16 = (pred[128,256]{1,0:T(8,128)(4,1)S(1)}, pred[128,256]{1,0:T(8,128)(4,1)}, u32[]{:S(2)}) copy-start(pred[128,256]{1,0:T(8,128)(4,1)} %copy-done.15) | copy-start | bytes 98308
  172.1 15.5 %collective-permute-start.35 = (bf16[400,256]{1,0:T(8,128)(2,1)S(1)}, bf16[400,256]{1,0:T(8,128)(2,1)S(1)}, u32[]{:S(2)}, u32[]{:S(2)}) collective-permute-start(bf16[400,256]{1,0:T(8,128)(2,1)S(1)} %pad_maximum_fusion.7), channel_id=1, source_target_pairs={{0,2},{2,0},{1,3},{3,1},{4,6},{6,4},{5,7},{7,5},{8,10},{10,8},{9,1... | collective-permute-start | bytes 614408 | tf_op jit(solution)/shard_map/ppermute | solution.py:371
  186.3 10.2 %slice-start = ((pred[128,256]{1,0:T(8,128)(4,1)}), pred[128,128]{1,0:T(8,128)(4,1)S(1)}, s32[]{:S(2)}) async-start(pred[128,256]{1,0:T(8,128)(4,1)} %copy-done.15), calls=%async_computation | async-start | bytes 32768 | tf_op jit(solution)/shard_map/slice | solution.py:404
  186.3 17.9 %slice-start.1 = ((s32[1536]{0:T(1024)}), s32[768]{0:T(1024)S(1)}, s32[]{:S(2)}) async-start(s32[1536]{0:T(1024)} %copy-done.19), calls=%async_computation.1 | async-start | bytes 8192 | tf_op jit(solution)/shard_map/slice | solution.py:414
  186.3 9.7 %collective-permute-start.32 = (bf16[384,512]{1,0:T(8,128)(2,1)S(1)}, bf16[384,512]{1,0:T(8,128)(2,1)S(1)}, u32[]{:S(2)}, u32[]{:S(2)}) collective-permute-start(bf16[384,512]{1,0:T(8,128)(2,1)S(1)} %get-tuple-element.121), channel_id=1, source_target_pairs={{2,0},{1,3},{6,4},{5,7},{10,8},{9,11},{14,12},{13,15},{18,16},{17,... | collective-permute-start | bytes 1179656 | tf_op jit(solution)/shard_map/ppermute | solution.py:380
  187.7 8.3 %collective-permute-start.36 = (bf16[400,256]{1,0:T(8,128)(2,1)S(1)}, bf16[400,256]{1,0:T(8,128)(2,1)S(1)}, u32[]{:S(2)}, u32[]{:S(2)}) collective-permute-start(bf16[400,256]{1,0:T(8,128)(2,1)S(1)} %pad_maximum_fusion.6), channel_id=1, source_target_pairs={{4,8},{8,4},{5,9},{9,5},{6,10},{10,6},{7,11},{11,7},{20,24},{24,20... | collective-permute-start | bytes 614408 | tf_op jit(solution)/shard_map/ppermute | solution.py:389
  196.7 3.7 %collective-permute-start.37 = (f32[2,3,128]{2,1,0:T(4,128)S(1)}, f32[2,3,128]{2,1,0:T(4,128)S(1)}, u32[]{:S(2)}, u32[]{:S(2)}) collective-permute-start(f32[2,3,128]{2,1,0:T(4,128)S(1)} %pad_maximum_fusion.9), channel_id=1, source_target_pairs={{0,2},{2,0},{1,3},{3,1},{4,6},{6,4},{5,7},{7,5},{8,10},{10,8},{9,1... | collective-permute-start | bytes 9224 | tf_op jit(solution)/shard_map/ppermute | solution.py:407
  200.3 3.7 %collective-permute-start.38 = (f32[2,6,128]{2,1,0:T(8,128)S(1)}, f32[2,6,128]{2,1,0:T(8,128)S(1)}, u32[]{:S(2)}, u32[]{:S(2)}) collective-permute-start(f32[2,6,128]{2,1,0:T(8,128)S(1)} %maximum_select_fusion.2), channel_id=1, source_target_pairs={{0,1},{1,0},{2,3},{3,2},{4,5},{5,4},{6,7},{7,6},{8,9},{9,8},{10,11... | collective-permute-start | bytes 18440 | tf_op jit(solution)/shard_map/ppermute | solution.py:407
  205.8 6.7 %collective-permute-start.39 = (f32[2,384]{1,0:T(2,128)S(1)}, f32[2,384]{1,0:T(2,128)S(1)}, u32[]{:S(2)}, u32[]{:S(2)}) collective-permute-start(f32[2,384]{1,0:T(2,128)S(1)} %pad_maximum_fusion.10), channel_id=1, source_target_pairs={{4,0},{8,12},{5,1},{9,13},{6,2},{10,14},{7,3},{11,15},{20,16},{24,... | collective-permute-start | bytes 9224 | tf_op jit(solution)/shard_map/ppermute | solution.py:421
  (21 other events, 78.6 us)

commit v2 on v1

--- a/solution.py
+++ b/solution.py
@@ -402,7 +402,6 @@
     keep = (tags[:-1, :, None] == both(tags)[:, None, :]) & at[None]
     sims = jnp.where(keep, sims, F32(-4.0))
     found = jnp.stack([jnp.max(sims, axis=2), jnp.max(sims[:, :, tile:], axis=1)])
-    found = after(found, came)
     for axis, index in (("tp", x), ("rep", c)):
         met = lax.ppermute(found, axis, SWAP)
         found = jnp.where(

time: 215 us -> 215 us (level); the launches traced: 214 us -> 212 us
  waiting for transfers between devices: 72.7 us -> 67.6 us
  starting transfers between devices: 67.4 us -> 71 us
    ppermute x1, waiting for transfers between devices: 7.5 us -> 3.01 us  [line_of_four(): lax.ppermute(late_rows, ('tp', 'rep'), [(2, 0), (1, 3)])]
    ppermute x1, waiting for transfers between devices: 0.01 us -> 3 us  [line_of_four(): lax.ppermute(early_rows, ('tp', 'rep'), [(0, 2), (3, 1)])]
    ppermute x2, starting transfers between devices: 2.98 us -> 5.98 us  [line_of_four(): met = lax.ppermute(found, axis, SWAP)]
    unnamed x58 -> x44, local copies, waits for them, and re-layouts: 11.3 us -> 10.8 us
where the time goes in v2:
time: 215 us; the launch traced here: 212 us
  starting transfers between devices  71 us (33%)
  waiting for transfers between devices  67.6 us (31%)
  Pallas kernels  35.7 us (17%)
  other arithmetic  21.1 us (10%)
  local copies, waits for them, and re-layouts  14.4 us (7%)
    ppermute x4, starting transfers between devices, inward(): return lax.ppermute(after(value, *gates), 'clus', OUT_IN)  21.5 us
    ppermute x3, waiting for transfers between devices, line_of_four(): lax.ppermute(names, 'clus', pairs)  15.8 us
    pallas_call x4, Pallas kernels, product(): pl.pallas_call(body, grid=(cols // block,), in_specs=[pl.BlockSpec((m, de...  13.7 us
    ppermute x2, waiting for transfers between devices, home(): lax.ppermute(value[1], ('clus', 'rep'), zc(near))  13.2 us
    pallas_call x2, Pallas kernels, late_part(): pl.pallas_call(body, grid_spec=pltpu.PrefetchScalarGridSpec(num_scalar_pr...  12.4 us
    ppermute x4, waiting for transfers between devices, inward(): return lax.ppermute(after(value, *gates), 'clus', OUT_IN)  11.6 us
    unnamed x44, local copies, waits for them, and re-layouts  10.8 us
    ppermute x2, waiting for transfers between devices, home(): lax.ppermute(value[3], ('clus', 'rep'), zc(far))  10.3 us
  transfers between devices with their start and end apart: 40, of which 10 were waited for; matrix products, arithmetic and copies ran while one was open for 12% of the time, Pallas kernels for 15%

profile of v2, /device:TPU:0, one launch (start us, length us, event | category | flops | bytes accessed | tf_op | source)
XLA Modules:
  0.0 211.7 jit_solution(16178470357944355040)
XLA Ops:
  0.6 5.0 %collective-permute-start = (bf16[384,2048]{1,0:T(8,128)(2,1)}, bf16[384,2048]{1,0:T(8,128)(2,1)S(1)}, u32[]{:S(2)}, u32[]{:S(2)}) collective-permute-start(bf16[384,2048]{1,0:T(8,128)(2,1)} %a.1), channel_id=1, source_target_pairs={{0,4},{12,8},{1,5},{13,9},{2,6},{14,10},{3,7},{15,11},{16,20},{28,... | collective-permute-start | bytes 4718600 | tf_op jit(solution)/shard_map/ppermute | solution.py:251
  5.7 1.8 collective-permute-start.1
  8.2 2.8 %collective-permute-start.2 = (s32[384]{0:T(512)S(1)}, s32[384]{0:T(512)S(1)}, u32[]{:S(2)}, u32[]{:S(2)}) collective-permute-start(s32[384]{0:T(512)S(1)} %reduce.1), channel_id=1, source_target_pairs={{0,4},{12,8},{1,5},{13,9},{2,6},{14,10},{3,7},{15,11},{16,20},{28,... | collective-permute-start | bytes 4616 | tf_op jit(solution)/shard_map/ppermute | solution.py:258
  11.7 4.0 %collective-permute-start.4 = (s32[384]{0:T(512)S(1)}, s32[384]{0:T(512)S(1)}, u32[]{:S(2)}, u32[]{:S(2)}) collective-permute-start(s32[384]{0:T(512)S(1)} %reduce.1), channel_id=1, source_target_pairs={{0,8},{12,4},{1,9},{13,5},{2,10},{14,6},{3,11},{15,7},{16,24},{28,... | collective-permute-start | bytes 4616 | tf_op jit(solution)/shard_map/ppermute | solution.py:258
  15.8 1.8 fusion.29
  17.6 1.5 pad_maximum_fusion.3
  19.2 1.7 copy-done.2
  20.8 3.0 %product.4.a.c = bf16[384,1024]{1,0:T(8,128)(2,1)S(1)} custom-call(bf16[384,2048]{1,0:T(8,128)(2,1)S(1)} %copy-done.4, bf16[2048,1024]{1,0:T(8,128)(2,1)S(1)} %copy-done.2), custom_call_target="tpu_custom_call" | custom-call | flops 1024 | bytes 1024 | tf_op jit(solution)/shard_map/product/pallas_call | solution.py:127
  23.8 15.7 %collective-permute-done.2 = s32[384]{0:T(512)S(1)} collective-permute-done((s32[384]{0:T(512)S(1)}, s32[384]{0:T(512)S(1)}, u32[]{:S(2)}, u32[]{:S(2)}) %collective-permute-start.2) | collective-permute-done | bytes 1568 | tf_op jit(solution)/shard_map/ppermute | solution.py:258
  40.2 1.5 collective-permute-start.6
  41.7 1.5 collective-permute-start.9
  43.2 7.3 %collective-permute-start.5 = (bf16[1024,512]{1,0:T(8,128)(2,1)}, bf16[1024,512]{1,0:T(8,128)(2,1)}, u32[]{:S(2)}, u32[]{:S(2)}) collective-permute-start(bf16[1024,512]{1,0:T(8,128)(2,1)} %get-tuple-element.58), channel_id=1, source_target_pairs={{0,4},{12,8},{1,5},{13,9},{2,6},{14,10},{3,7},{15,11},{16,20},{28,... | collective-permute-start | bytes 3145736 | tf_op jit(solution)/shard_map/ppermute | solution.py:251
  51.7 1.6 collective-permute-start.8
  53.3 4.9 %product.6.a.c = bf16[384,1024]{1,0:T(8,128)(2,1)} custom-call(bf16[384,2048]{1,0:T(8,128)(2,1)} %collective-permute-done.1.a, bf16[2048,1024]{1,0:T(8,128)(2,1)S(1)} %copy-done.2), custom_call_target="tpu_custom_call" | custom-call | flops 1024 | bytes 1024 | tf_op jit(solution)/shard_map/product/pallas_call | solution.py:127
  58.2 1.6 collective-permute-start.11
  59.7 3.0 %product.5.a.c = bf16[384,1024]{1,0:T(8,128)(2,1)S(1)} custom-call(bf16[384,2048]{1,0:T(8,128)(2,1)S(1)} %collective-permute-done.a, bf16[2048,1024]{1,0:T(8,128)(2,1)S(1)} %copy-done.2), custom_call_target="tpu_custom_call" | custom-call | flops 1024 | bytes 1024 | tf_op jit(solution)/shard_map/product/pallas_call | solution.py:127
  62.7 1.6 collective-permute-start.10
  64.3 1.6 constant_dynamic-update-slice_fusion.4
  66.7 1.3 fold.6
  68.9 1.5 fold.8
  71.4 1.4 fold.7
  72.9 6.1 %collective-permute-start.12 = (bf16[1024,512]{1,0:T(8,128)(2,1)S(1)}, bf16[1024,512]{1,0:T(8,128)(2,1)}, u32[]{:S(2)}, u32[]{:S(2)}) collective-permute-start(bf16[1024,512]{1,0:T(8,128)(2,1)S(1)} %copy-done.11), channel_id=1, source_target_pairs={{0,4},{12,8},{1,5},{13,9},{2,6},{14,10},{3,7},{15,11},{16,20},{28,... | collective-permute-start | bytes 3145736 | tf_op jit(solution)/shard_map/ppermute | solution.py:251
  79.0 1.5 collective-permute-start.13
  80.5 1.6 constant_dynamic-update-slice_fusion.2
  83.7 3.0 %convert_reduce_fusion = s32[1536]{0:T(1024)S(1)} fusion(s32[1536]{0:T(1024)S(1)} %add.151, s32[1536]{0:T(1024)S(1)} %copy-done.15), kind=kLoop, calls=%fused_computation.2 | loop fusion | flops 16513536 | bytes 18432 | tf_op jit(solution)/shard_map/reduce_sum | solution.py:291
  87.8 10.1 %collective-permute-done.12.own = bf16[1024,512]{1,0:T(8,128)(2,1)} collective-permute-done((bf16[1024,512]{1,0:T(8,128)(2,1)S(1)}, bf16[1024,512]{1,0:T(8,128)(2,1)}, u32[]{:S(2)}, u32[]{:S(2)}) %collective-permute-start.12) | collective-permute-done | bytes 1048608 | tf_op jit(solution)/shard_map/ppermute | solution.py:251
  97.9 4.4 %collective-permute-done.13.other = bf16[1024,512]{1,0:T(8,128)(2,1)S(1)} collective-permute-done((bf16[1024,512]{1,0:T(8,128)(2,1)}, bf16[1024,512]{1,0:T(8,128)(2,1)S(1)}, u32[]{:S(2)}, u32[]{:S(2)}) %collective-permute-start.13) | collective-permute-done | bytes 1048608 | tf_op jit(solution)/shard_map/ppermute | solution.py:248
  102.3 1.5 collective-permute-start.21
  105.0 1.7 collective-permute-start.24
  108.0 6.9 %late_part.2.a.c = bf16[1536,512]{1,0:T(8,128)(2,1)S(1)} custom-call(s32[1]{0:T(128)} %bitcast.1._, bf16[1536,2048]{1,0:T(8,128)(2,1)S(1)} %constant_dynamic-update-slice_fusion.a.b, bf16[1536,2048]{1,0:T(8,128)(2,1)S(1)} %constant_dynamic-update-slice_fusion.a.b, bf16[1024,512]{1,0:T(8,128)(2,1)} %collective-permute-done.5.own, ...), custom_call_target="tpu_custom_call" | custom-call | flops 1024 | bytes 1024 | tf_op jit(solution)/shard_map/late_part/pallas_call | solution.py:99
  114.9 1.3 pad_maximum_fusion.1.a
  116.3 3.0 %product.7.a.c = bf16[384,1024]{1,0:T(8,128)(2,1)S(1)} custom-call(bf16[384,2048]{1,0:T(8,128)(2,1)S(1)} %pad_maximum_fusion.1.a, bf16[2048,1024]{1,0:T(8,128)(2,1)S(1)} %copy-done.3), custom_call_target="tpu_custom_call" | custom-call | flops 1024 | bytes 1024 | tf_op jit(solution)/shard_map/product/pallas_call | solution.py:127
  120.8 3.2 %collective-permute-start.19 = (bf16[384,512]{1,0:T(8,128)(2,1)}, bf16[384,512]{1,0:T(8,128)(2,1)S(1)}, u32[]{:S(2)}, u32[]{:S(2)}) collective-permute-start(bf16[384,512]{1,0:T(8,128)(2,1)} %get-tuple-element.89), channel_id=1, source_target_pairs={{0,8},{12,4},{1,9},{13,5},{2,10},{14,6},{3,11},{15,7},{16,24},{28,... | collective-permute-start | bytes 1179656 | tf_op jit(solution)/shard_map/ppermute | solution.py:305
  124.8 3.1 %collective-permute-start.17 = (bf16[384,512]{1,0:T(8,128)(2,1)S(1)}, bf16[384,512]{1,0:T(8,128)(2,1)S(1)}, u32[]{:S(2)}, u32[]{:S(2)}) collective-permute-start(bf16[384,512]{1,0:T(8,128)(2,1)S(1)} %get-tuple-element.87), channel_id=1, source_target_pairs={{0,4},{12,8},{1,5},{13,9},{2,6},{14,10},{3,7},{15,11},{16,20},{28,... | collective-permute-start | bytes 1179656 | tf_op jit(solution)/shard_map/ppermute | solution.py:251
  128.7 2.8 %copy-done.1 = bf16[1536,2048]{1,0:T(8,128)(2,1)S(1)} copy-done((bf16[1536,2048]{1,0:T(8,128)(2,1)S(1)}, bf16[1536,2048]{1,0:T(8,128)(2,1)}, u32[]{:S(2)}) %copy-start.1) | copy-done | bytes 6291480
  131.5 5.5 %late_part.3.a.c = bf16[1536,512]{1,0:T(8,128)(2,1)S(1)} custom-call(s32[1]{0:T(128)} %bitcast.1._, bf16[1536,2048]{1,0:T(8,128)(2,1)S(1)} %copy-done.1, bf16[1536,2048]{1,0:T(8,128)(2,1)S(1)} %copy-done.1, bf16[1024,512]{1,0:T(8,128)(2,1)} %collective-permute-done.12.own, bf16[1024,512]{1,0:T(8,128)(2,1)} %collective-permute-done.21.other), custom_call_target="tpu_custom_call" | custom-call | flops 1024 | bytes 1024 | tf_op jit(solution)/shard_map/late_part/pallas_call | solution.py:99
  137.8 1.6 maximum_add_fusion.1
  140.6 1.4 collective-permute-done.17
  148.9 10.3 %collective-permute-done.28 = bf16[384,512]{1,0:T(8,128)(2,1)S(1)} collective-permute-done((bf16[384,512]{1,0:T(8,128)(2,1)S(1)}, bf16[384,512]{1,0:T(8,128)(2,1)S(1)}, u32[]{:S(2)}, u32[]{:S(2)}) %collective-permute-start.28) | collective-permute-done | bytes 393248 | tf_op jit(solution)/shard_map/ppermute | solution.py:327
  160.3 3.6 %tile_gram.1 = (bf16[12,128,256]{2,1,0:T(8,128)(2,1)S(1)}, f32[12,128]{1,0:T(8,128)S(1)}) custom-call(s32[1]{0:T(128)} %bitcast.9.flag, s32[1,1536]{1,0:T(1,128)S(1)} %reshape.142.place, bf16[1536,512]{1,0:T(8,128)(2,1)S(1)} %pad_maximum_fusion.late, bf16[1536,512]{1,0:T(8,128)(2,1)S(1)} %fusion.1.early), custom_call_target="tpu_custom_call" | custom-call | flops 1024 | bytes 1024 | tf_op jit(solution)/shard_map/tile_gram/pallas_call | solution.py:200
  169.7 13.2 %collective-permute-done.29 = bf16[384,512]{1,0:T(8,128)(2,1)S(1)} collective-permute-done((bf16[384,512]{1,0:T(8,128)(2,1)S(1)}, bf16[384,512]{1,0:T(8,128)(2,1)S(1)}, u32[]{:S(2)}, u32[]{:S(2)}) %collective-permute-start.29) | collective-permute-done | bytes 393248 | tf_op jit(solution)/shard_map/ppermute | solution.py:325
  185.3 2.9 %collective-permute-done.37 = f32[2,3,128]{2,1,0:T(4,128)S(1)} collective-permute-done((f32[2,3,128]{2,1,0:T(4,128)S(1)}, f32[2,3,128]{2,1,0:T(4,128)S(1)}, u32[]{:S(2)}, u32[]{:S(2)}) %collective-permute-start.37) | collective-permute-done | bytes 3104 | tf_op jit(solution)/shard_map/ppermute | solution.py:406
  188.3 5.2 %collective-permute-start.38 = (f32[2,6,128]{2,1,0:T(8,128)S(1)}, f32[2,6,128]{2,1,0:T(8,128)S(1)}, u32[]{:S(2)}, u32[]{:S(2)}) collective-permute-start(f32[2,6,128]{2,1,0:T(8,128)S(1)} %maximum_select_fusion.2), channel_id=1, source_target_pairs={{0,1},{1,0},{2,3},{3,2},{4,5},{5,4},{6,7},{7,6},{8,9},{9,8},{10,11... | collective-permute-start | bytes 18440 | tf_op jit(solution)/shard_map/ppermute | solution.py:406
  193.5 2.6 %collective-permute-start.33 = (bf16[384,512]{1,0:T(8,128)(2,1)S(1)}, bf16[384,512]{1,0:T(8,128)(2,1)S(1)}, u32[]{:S(2)}, u32[]{:S(2)}) collective-permute-start(bf16[384,512]{1,0:T(8,128)(2,1)S(1)} %slice_select_fusion), channel_id=1, source_target_pairs={{0,2},{3,1},{4,6},{7,5},{8,10},{11,9},{12,14},{15,13},{16,18},{19,... | collective-permute-start | bytes 1179656 | tf_op jit(solution)/shard_map/ppermute | solution.py:380
  197.5 1.6 select_reduce_fusion.2
  200.4 3.0 %collective-permute-done.33 = bf16[384,512]{1,0:T(8,128)(2,1)S(1)} collective-permute-done((bf16[384,512]{1,0:T(8,128)(2,1)S(1)}, bf16[384,512]{1,0:T(8,128)(2,1)S(1)}, u32[]{:S(2)}, u32[]{:S(2)}) %collective-permute-start.33) | collective-permute-done | bytes 393248 | tf_op jit(solution)/shard_map/ppermute | solution.py:380
  203.4 3.0 %collective-permute-done.32 = bf16[384,512]{1,0:T(8,128)(2,1)S(1)} collective-permute-done((bf16[384,512]{1,0:T(8,128)(2,1)S(1)}, bf16[384,512]{1,0:T(8,128)(2,1)S(1)}, u32[]{:S(2)}, u32[]{:S(2)}) %collective-permute-start.32) | collective-permute-done | bytes 393248 | tf_op jit(solution)/shard_map/ppermute | solution.py:380
  206.6 3.4 %collective-permute-done.39 = f32[2,384]{1,0:T(2,128)S(1)} collective-permute-done((f32[2,384]{1,0:T(2,128)S(1)}, f32[2,384]{1,0:T(2,128)S(1)}, u32[]{:S(2)}, u32[]{:S(2)}) %collective-permute-start.39) | collective-permute-done | bytes 3104 | tf_op jit(solution)/shard_map/ppermute | solution.py:420
  (169 shorter events, 36.2 us)
Async XLA Ops:
  0.6 39.5 %collective-permute-start = (bf16[384,2048]{1,0:T(8,128)(2,1)}, bf16[384,2048]{1,0:T(8,128)(2,1)S(1)}, u32[]{:S(2)}, u32[]{:S(2)}) collective-permute-start(bf16[384,2048]{1,0:T(8,128)(2,1)} %a.1), channel_id=1, source_target_pairs={{0,4},{12,8},{1,5},{13,9},{2,6},{14,10},{3,7},{15,11},{16,20},{28,... | collective-permute-start | bytes 4718600 | tf_op jit(solution)/shard_map/ppermute | solution.py:251
  5.7 34.5 %collective-permute-start.1 = (bf16[384,2048]{1,0:T(8,128)(2,1)}, bf16[384,2048]{1,0:T(8,128)(2,1)}, u32[]{:S(2)}, u32[]{:S(2)}) collective-permute-start(bf16[384,2048]{1,0:T(8,128)(2,1)} %a.1), channel_id=1, source_target_pairs={{4,8},{8,4},{5,9},{9,5},{6,10},{10,6},{7,11},{11,7},{20,24},{24,20... | collective-permute-start | bytes 4718600 | tf_op jit(solution)/shard_map/ppermute | solution.py:256
  8.2 31.4 %collective-permute-start.2 = (s32[384]{0:T(512)S(1)}, s32[384]{0:T(512)S(1)}, u32[]{:S(2)}, u32[]{:S(2)}) collective-permute-start(s32[384]{0:T(512)S(1)} %reduce.1), channel_id=1, source_target_pairs={{0,4},{12,8},{1,5},{13,9},{2,6},{14,10},{3,7},{15,11},{16,20},{28,... | collective-permute-start | bytes 4616 | tf_op jit(solution)/shard_map/ppermute | solution.py:258
  11.1 28.5 %collective-permute-start.3 = (s32[384]{0:T(512)S(1)}, s32[384]{0:T(512)S(1)}, u32[]{:S(2)}, u32[]{:S(2)}) collective-permute-start(s32[384]{0:T(512)S(1)} %reduce.1), channel_id=1, source_target_pairs={{4,8},{8,4},{5,9},{9,5},{6,10},{10,6},{7,11},{11,7},{20,24},{24,20... | collective-permute-start | bytes 4616 | tf_op jit(solution)/shard_map/ppermute | solution.py:258
  11.7 27.8 %collective-permute-start.4 = (s32[384]{0:T(512)S(1)}, s32[384]{0:T(512)S(1)}, u32[]{:S(2)}, u32[]{:S(2)}) collective-permute-start(s32[384]{0:T(512)S(1)} %reduce.1), channel_id=1, source_target_pairs={{0,8},{12,4},{1,9},{13,5},{2,10},{14,6},{3,11},{15,7},{16,24},{28,... | collective-permute-start | bytes 4616 | tf_op jit(solution)/shard_map/ppermute | solution.py:258
  40.2 13.1 %collective-permute-start.6 = (bf16[384,512]{1,0:T(8,128)(2,1)S(1)}, bf16[384,512]{1,0:T(8,128)(2,1)S(1)}, u32[]{:S(2)}, u32[]{:S(2)}) collective-permute-start(bf16[384,512]{1,0:T(8,128)(2,1)S(1)} %constant_dynamic-slice_fusion.4), channel_id=1, source_target_pairs={{0,2},{2,0},{1,3},{3,1},{4,6},{6,4},{5,7},{7,5},{8,10},{10,8},{9,1... | collective-permute-start | bytes 1179656 | tf_op jit(solution)/shard_map/ppermute | solution.py:273
  41.7 24.3 %collective-permute-start.9 = (bf16[384,1024]{1,0:T(8,128)(2,1)S(1)}, bf16[384,1024]{1,0:T(8,128)(2,1)}, u32[]{:S(2)}, u32[]{:S(2)}) collective-permute-start(bf16[384,1024]{1,0:T(8,128)(2,1)S(1)} %product.4.a.c), channel_id=1, source_target_pairs={{4,5},{9,8},{6,7},{11,10},{20,21},{25,24},{22,23},{27,26}} | collective-permute-start | bytes 2359304 | tf_op jit(solution)/shard_map/ppermute | solution.py:242
  43.2 29.6 %collective-permute-start.5 = (bf16[1024,512]{1,0:T(8,128)(2,1)}, bf16[1024,512]{1,0:T(8,128)(2,1)}, u32[]{:S(2)}, u32[]{:S(2)}) collective-permute-start(bf16[1024,512]{1,0:T(8,128)(2,1)} %get-tuple-element.58), channel_id=1, source_target_pairs={{0,4},{12,8},{1,5},{13,9},{2,6},{14,10},{3,7},{15,11},{16,20},{28,... | collective-permute-start | bytes 3145736 | tf_op jit(solution)/shard_map/ppermute | solution.py:251
  51.7 21.1 %collective-permute-start.8 = (bf16[192,2048]{1,0:T(8,128)(2,1)}, bf16[192,2048]{1,0:T(8,128)(2,1)}, u32[]{:S(2)}, u32[]{:S(2)}) collective-permute-start(bf16[192,2048]{1,0:T(8,128)(2,1)} %get-tuple-element.133), channel_id=1, source_target_pairs={{4,8},{8,4},{5,9},{9,5},{6,10},{10,6},{7,11},{11,7},{20,24},{24,20... | collective-permute-start | bytes 2359304 | tf_op jit(solution)/shard_map/ppermute | solution.py:272
  58.2 10.8 %collective-permute-start.11 = (bf16[384,1024]{1,0:T(8,128)(2,1)}, bf16[384,1024]{1,0:T(8,128)(2,1)}, u32[]{:S(2)}, u32[]{:S(2)}) collective-permute-start(bf16[384,1024]{1,0:T(8,128)(2,1)} %product.6.a.c), channel_id=1, source_target_pairs={{4,5},{9,8},{6,7},{11,10},{20,21},{25,24},{22,23},{27,26}} | collective-permute-start | bytes 2359304 | tf_op jit(solution)/shard_map/ppermute | solution.py:242
  62.7 8.7 %collective-permute-start.10 = (bf16[384,1024]{1,0:T(8,128)(2,1)S(1)}, bf16[384,1024]{1,0:T(8,128)(2,1)}, u32[]{:S(2)}, u32[]{:S(2)}) collective-permute-start(bf16[384,1024]{1,0:T(8,128)(2,1)S(1)} %product.5.a.c), channel_id=1, source_target_pairs={{4,5},{9,8},{6,7},{11,10},{20,21},{25,24},{22,23},{27,26}} | collective-permute-start | bytes 2359304 | tf_op jit(solution)/shard_map/ppermute | solution.py:242
  66.0 6.8 %collective-permute-start.7 = (f32[1024]{0:T(1024)S(1)}, f32[1024]{0:T(1024)S(1)}, u32[]{:S(2)}, u32[]{:S(2)}) collective-permute-start(f32[1024]{0:T(1024)S(1)} %copy-done.16), channel_id=1, source_target_pairs={{0,2},{2,0},{1,3},{3,1},{4,6},{6,4},{5,7},{7,5},{8,10},{10,8},{9,1... | collective-permute-start | bytes 12296 | tf_op jit(solution)/shard_map/ppermute | solution.py:274
  72.8 11.0 %copy-start.9 = (f32[384,512]{1,0:T(8,128)}, f32[384,512]{1,0:T(8,128)S(1)}, u32[]{:S(2)}) copy-start(f32[384,512]{1,0:T(8,128)S(1)} %get-tuple-element.99) | copy-start | bytes 2359300
  72.8 9.3 %copy-start.14 = (bf16[192,2048]{1,0:T(8,128)(2,1)S(1)}, bf16[192,2048]{1,0:T(8,128)(2,1)}, u32[]{:S(2)}) copy-start(bf16[192,2048]{1,0:T(8,128)(2,1)} %get-tuple-element.132) | copy-start | bytes 2359300
  72.8 10.0 %copy-start.13 = (bf16[384,1024]{1,0:T(8,128)(2,1)S(1)}, bf16[384,1024]{1,0:T(8,128)(2,1)}, u32[]{:S(2)}) copy-start(bf16[384,1024]{1,0:T(8,128)(2,1)} %param.8) | copy-start | bytes 2359300
  72.8 10.0 %copy-start.17 = (f32[1024]{0:T(1024)}, f32[1024]{0:T(1024)S(1)}, u32[]{:S(2)}) copy-start(f32[1024]{0:T(1024)S(1)} %collective-permute-done.7) | copy-start | bytes 12292
  72.8 10.9 %copy-start.15 = (s32[1536]{0:T(1024)S(1)}, s32[1536]{0:T(1024)}, u32[]{:S(2)}) copy-start(s32[1536]{0:T(1024)} %pad_add_fusion) | copy-start | bytes 18436
  72.9 25.0 %collective-permute-start.12 = (bf16[1024,512]{1,0:T(8,128)(2,1)S(1)}, bf16[1024,512]{1,0:T(8,128)(2,1)}, u32[]{:S(2)}, u32[]{:S(2)}) collective-permute-start(bf16[1024,512]{1,0:T(8,128)(2,1)S(1)} %copy-done.11), channel_id=1, source_target_pairs={{0,4},{12,8},{1,5},{13,9},{2,6},{14,10},{3,7},{15,11},{16,20},{28,... | collective-permute-start | bytes 3145736 | tf_op jit(solution)/shard_map/ppermute | solution.py:251
  79.0 23.3 %collective-permute-start.13 = (bf16[1024,512]{1,0:T(8,128)(2,1)}, bf16[1024,512]{1,0:T(8,128)(2,1)S(1)}, u32[]{:S(2)}, u32[]{:S(2)}) collective-permute-start(bf16[1024,512]{1,0:T(8,128)(2,1)} %collective-permute-done.5.own), channel_id=1, source_target_pairs={{0,16},{16,0},{1,17},{17,1},{2,18},{18,2},{3,19},{19,3},{4,20},{20... | collective-permute-start | bytes 3145736 | tf_op jit(solution)/shard_map/ppermute | solution.py:248
  82.1 5.7 %collective-permute-start.14 = (bf16[192,2048]{1,0:T(8,128)(2,1)S(1)}, bf16[192,2048]{1,0:T(8,128)(2,1)S(1)}, u32[]{:S(2)}, u32[]{:S(2)}) collective-permute-start(bf16[192,2048]{1,0:T(8,128)(2,1)S(1)} %copy-done.14), channel_id=1, source_target_pairs={{4,8},{8,4},{5,9},{9,5},{6,10},{10,6},{7,11},{11,7},{20,24},{24,20... | collective-permute-start | bytes 2359304 | tf_op jit(solution)/shard_map/ppermute | solution.py:282
  102.3 25.7 %collective-permute-start.21 = (bf16[1024,512]{1,0:T(8,128)(2,1)}, bf16[1024,512]{1,0:T(8,128)(2,1)}, u32[]{:S(2)}, u32[]{:S(2)}) collective-permute-start(bf16[1024,512]{1,0:T(8,128)(2,1)} %collective-permute-done.12.own), channel_id=1, source_target_pairs={{0,16},{16,0},{1,17},{17,1},{2,18},{18,2},{3,19},{19,3},{4,20},{20... | collective-permute-start | bytes 3145736 | tf_op jit(solution)/shard_map/ppermute | solution.py:248
  105.0 32.0 %collective-permute-start.24 = (bf16[1152,512]{1,0:T(8,128)(2,1)}, bf16[1152,512]{1,0:T(8,128)(2,1)}, u32[]{:S(2)}, u32[]{:S(2)}) collective-permute-start(bf16[1152,512]{1,0:T(8,128)(2,1)} %pad_maximum_fusion.2), channel_id=1, source_target_pairs={{5,7},{7,5},{8,10},{10,8},{21,23},{23,21},{24,26},{26,24}} | collective-permute-start | bytes 3538952 | tf_op jit(solution)/shard_map/ppermute | solution.py:245
  108.0 7.0 %copy-start = (bf16[1536,2048]{1,0:T(8,128)(2,1)}, bf16[1536,2048]{1,0:T(8,128)(2,1)S(1)}, u32[]{:S(2)}) copy-start(bf16[1536,2048]{1,0:T(8,128)(2,1)S(1)} %constant_dynamic-update-slice_fusion.a.b) | copy-start | bytes 18874372
  108.0 8.3 %copy-start.3 = (bf16[2048,1024]{1,0:T(8,128)(2,1)S(1)}, bf16[2048,1024]{1,0:T(8,128)(2,1)}, u32[]{:S(2)}) copy-start(bf16[2048,1024]{1,0:T(8,128)(2,1)} %b.7) | copy-start | bytes 12582916
  119.2 5.5 %collective-permute-start.20 = (bf16[384,1024]{1,0:T(8,128)(2,1)S(1)}, bf16[384,1024]{1,0:T(8,128)(2,1)S(1)}, u32[]{:S(2)}, u32[]{:S(2)}) collective-permute-start(bf16[384,1024]{1,0:T(8,128)(2,1)S(1)} %product.7.a.c), channel_id=1, source_target_pairs={{4,5},{9,8},{6,7},{11,10},{20,21},{25,24},{22,23},{27,26}} | collective-permute-start | bytes 2359304 | tf_op jit(solution)/shard_map/ppermute | solution.py:242
  120.8 21.2 %collective-permute-start.19 = (bf16[384,512]{1,0:T(8,128)(2,1)}, bf16[384,512]{1,0:T(8,128)(2,1)S(1)}, u32[]{:S(2)}, u32[]{:S(2)}) collective-permute-start(bf16[384,512]{1,0:T(8,128)(2,1)} %get-tuple-element.89), channel_id=1, source_target_pairs={{0,8},{12,4},{1,9},{13,5},{2,10},{14,6},{3,11},{15,7},{16,24},{28,... | collective-permute-start | bytes 1179656 | tf_op jit(solution)/shard_map/ppermute | solution.py:305
  124.1 16.5 %collective-permute-start.18 = (bf16[384,512]{1,0:T(8,128)(2,1)}, bf16[384,512]{1,0:T(8,128)(2,1)S(1)}, u32[]{:S(2)}, u32[]{:S(2)}) collective-permute-start(bf16[384,512]{1,0:T(8,128)(2,1)} %get-tuple-element.89), channel_id=1, source_target_pairs={{4,8},{8,4},{5,9},{9,5},{6,10},{10,6},{7,11},{11,7},{20,24},{24,20... | collective-permute-start | bytes 1179656 | tf_op jit(solution)/shard_map/ppermute | solution.py:306
  124.8 17.2 %collective-permute-start.17 = (bf16[384,512]{1,0:T(8,128)(2,1)S(1)}, bf16[384,512]{1,0:T(8,128)(2,1)S(1)}, u32[]{:S(2)}, u32[]{:S(2)}) collective-permute-start(bf16[384,512]{1,0:T(8,128)(2,1)S(1)} %get-tuple-element.87), channel_id=1, source_target_pairs={{0,4},{12,8},{1,5},{13,9},{2,6},{14,10},{3,7},{15,11},{16,20},{28,... | collective-permute-start | bytes 1179656 | tf_op jit(solution)/shard_map/ppermute | solution.py:251
  128.0 11.4 %collective-permute-start.25 = (bf16[384,512]{1,0:T(8,128)(2,1)S(1)}, bf16[384,512]{1,0:T(8,128)(2,1)S(1)}, u32[]{:S(2)}, u32[]{:S(2)}) collective-permute-start(bf16[384,512]{1,0:T(8,128)(2,1)S(1)} %get-tuple-element.93), channel_id=1, source_target_pairs={{5,7},{7,5},{8,10},{10,8},{21,23},{23,21},{24,26},{26,24}} | collective-permute-start | bytes 1179656 | tf_op jit(solution)/shard_map/ppermute | solution.py:245
  131.5 6.3 %copy-start.10 = (f32[384,512]{1,0:T(8,128)S(1)}, f32[384,512]{1,0:T(8,128)}, u32[]{:S(2)}) copy-start(f32[384,512]{1,0:T(8,128)} %copy-done.9) | copy-start | bytes 2359300
  137.0 8.4 %collective-permute-start.22 = (bf16[1536,512]{1,0:T(8,128)(2,1)S(1)}, bf16[1536,512]{1,0:T(8,128)(2,1)S(1)}, u32[]{:S(2)}, u32[]{:S(2)}) collective-permute-start(bf16[1536,512]{1,0:T(8,128)(2,1)S(1)} %late_part.3.a.c), channel_id=1, source_target_pairs={{5,4},{8,9},{7,6},{10,11},{21,20},{24,25},{23,22},{26,27}} | collective-permute-start | bytes 4718600 | tf_op jit(solution)/shard_map/ppermute | solution.py:242
  139.5 7.9 %collective-permute-start.15 = (bf16[1536,512]{1,0:T(8,128)(2,1)S(1)}, bf16[1536,512]{1,0:T(8,128)(2,1)S(1)}, u32[]{:S(2)}, u32[]{:S(2)}) collective-permute-start(bf16[1536,512]{1,0:T(8,128)(2,1)S(1)} %late_part.2.a.c), channel_id=1, source_target_pairs={{5,4},{8,9},{7,6},{10,11},{21,20},{24,25},{23,22},{26,27}} | collective-permute-start | bytes 4718600 | tf_op jit(solution)/shard_map/ppermute | solution.py:242
  142.7 6.2 %collective-permute-start.26 = (bf16[384,512]{1,0:T(8,128)(2,1)S(1)}, bf16[384,512]{1,0:T(8,128)(2,1)S(1)}, u32[]{:S(2)}, u32[]{:S(2)}) collective-permute-start(bf16[384,512]{1,0:T(8,128)(2,1)S(1)} %get-tuple-element.131), channel_id=1, source_target_pairs={{8,12},{5,1},{10,14},{7,3},{24,28},{21,17},{26,30},{23,19}} | collective-permute-start | bytes 1179656 | tf_op jit(solution)/shard_map/ppermute | solution.py:325
  143.4 5.5 %collective-permute-start.27 = (bf16[384,512]{1,0:T(8,128)(2,1)S(1)}, bf16[384,512]{1,0:T(8,128)(2,1)S(1)}, u32[]{:S(2)}, u32[]{:S(2)}) collective-permute-start(bf16[384,512]{1,0:T(8,128)(2,1)S(1)} %get-tuple-element.129), channel_id=1, source_target_pairs={{8,4},{5,9},{10,6},{7,11},{24,20},{21,25},{26,22},{23,27}} | collective-permute-start | bytes 1179656 | tf_op jit(solution)/shard_map/ppermute | solution.py:326
  144.1 15.1 %collective-permute-start.28 = (bf16[384,512]{1,0:T(8,128)(2,1)S(1)}, bf16[384,512]{1,0:T(8,128)(2,1)S(1)}, u32[]{:S(2)}, u32[]{:S(2)}) collective-permute-start(bf16[384,512]{1,0:T(8,128)(2,1)S(1)} %get-tuple-element.130), channel_id=1, source_target_pairs={{8,0},{5,13},{10,2},{7,15},{24,16},{21,29},{26,18},{23,31}} | collective-permute-start | bytes 1179656 | tf_op jit(solution)/shard_map/ppermute | solution.py:327
  146.2 13.1 %collective-permute-start.23 = (bf16[1536,256]{1,0:T(8,128)(2,1)S(1)}, bf16[1536,256]{1,0:T(8,128)(2,1)S(1)}, u32[]{:S(2)}, u32[]{:S(2)}) collective-permute-start(bf16[1536,256]{1,0:T(8,128)(2,1)S(1)} %get-tuple-element.97), channel_id=1, source_target_pairs={{4,6},{6,4},{9,11},{11,9},{20,22},{22,20},{25,27},{27,25}} | collective-permute-start | bytes 2359304 | tf_op jit(solution)/shard_map/ppermute | solution.py:245
  148.2 11.3 %collective-permute-start.16 = (bf16[1536,256]{1,0:T(8,128)(2,1)S(1)}, bf16[1536,256]{1,0:T(8,128)(2,1)S(1)}, u32[]{:S(2)}, u32[]{:S(2)}) collective-permute-start(bf16[1536,256]{1,0:T(8,128)(2,1)S(1)} %get-tuple-element.86), channel_id=1, source_target_pairs={{4,6},{6,4},{9,11},{11,9},{20,22},{22,20},{25,27},{27,25}} | collective-permute-start | bytes 2359304 | tf_op jit(solution)/shard_map/ppermute | solution.py:245
  164.1 3.0 %collective-permute-start.34 = (bf16[784,256]{1,0:T(8,128)(2,1)S(1)}, bf16[784,256]{1,0:T(8,128)(2,1)}, u32[]{:S(2)}, u32[]{:S(2)}) collective-permute-start(bf16[784,256]{1,0:T(8,128)(2,1)S(1)} %pad_maximum_fusion.5), channel_id=1, source_target_pairs={{0,1},{1,0},{2,3},{3,2},{4,5},{5,4},{6,7},{7,6},{8,9},{9,8},{10,11... | collective-permute-start | bytes 1204232 | tf_op jit(solution)/shard_map/ppermute | solution.py:371
  164.4 18.5 %collective-permute-start.29 = (bf16[384,512]{1,0:T(8,128)(2,1)S(1)}, bf16[384,512]{1,0:T(8,128)(2,1)S(1)}, u32[]{:S(2)}, u32[]{:S(2)}) collective-permute-start(bf16[384,512]{1,0:T(8,128)(2,1)S(1)} %get-tuple-element.127), channel_id=1, source_target_pairs={{4,0},{9,13},{6,2},{11,15},{20,16},{25,29},{22,18},{27,31}} | collective-permute-start | bytes 1179656 | tf_op jit(solution)/shard_map/ppermute | solution.py:325
  165.7 17.2 %collective-permute-start.30 = (bf16[384,512]{1,0:T(8,128)(2,1)S(1)}, bf16[384,512]{1,0:T(8,128)(2,1)S(1)}, u32[]{:S(2)}, u32[]{:S(2)}) collective-permute-start(bf16[384,512]{1,0:T(8,128)(2,1)S(1)} %get-tuple-element.126), channel_id=1, source_target_pairs={{4,8},{9,5},{6,10},{11,7},{20,24},{25,21},{22,26},{27,23}} | collective-permute-start | bytes 1179656 | tf_op jit(solution)/shard_map/ppermute | solution.py:326
  166.3 16.5 %collective-permute-start.31 = (bf16[384,512]{1,0:T(8,128)(2,1)S(1)}, bf16[384,512]{1,0:T(8,128)(2,1)S(1)}, u32[]{:S(2)}, u32[]{:S(2)}) collective-permute-start(bf16[384,512]{1,0:T(8,128)(2,1)S(1)} %get-tuple-element.128), channel_id=1, source_target_pairs={{4,12},{9,1},{6,14},{11,3},{20,28},{25,17},{22,30},{27,19}} | collective-permute-start | bytes 1179656 | tf_op jit(solution)/shard_map/ppermute | solution.py:327
  168.9 14.2 %collective-permute-start.35 = (bf16[400,256]{1,0:T(8,128)(2,1)S(1)}, bf16[400,256]{1,0:T(8,128)(2,1)S(1)}, u32[]{:S(2)}, u32[]{:S(2)}) collective-permute-start(bf16[400,256]{1,0:T(8,128)(2,1)S(1)} %pad_maximum_fusion.7), channel_id=1, source_target_pairs={{0,2},{2,0},{1,3},{3,1},{4,6},{6,4},{5,7},{7,5},{8,10},{10,8},{9,1... | collective-permute-start | bytes 614408 | tf_op jit(solution)/shard_map/ppermute | solution.py:371
  183.3 0.7 collective-permute-start.36
  184.6 3.7 %collective-permute-start.37 = (f32[2,3,128]{2,1,0:T(4,128)S(1)}, f32[2,3,128]{2,1,0:T(4,128)S(1)}, u32[]{:S(2)}, u32[]{:S(2)}) collective-permute-start(f32[2,3,128]{2,1,0:T(4,128)S(1)} %pad_maximum_fusion.9), channel_id=1, source_target_pairs={{0,2},{2,0},{1,3},{3,1},{4,6},{6,4},{5,7},{7,5},{8,10},{10,8},{9,1... | collective-permute-start | bytes 9224 | tf_op jit(solution)/shard_map/ppermute | solution.py:406
  188.3 9.1 %collective-permute-start.38 = (f32[2,6,128]{2,1,0:T(8,128)S(1)}, f32[2,6,128]{2,1,0:T(8,128)S(1)}, u32[]{:S(2)}, u32[]{:S(2)}) collective-permute-start(f32[2,6,128]{2,1,0:T(8,128)S(1)} %maximum_select_fusion.2), channel_id=1, source_target_pairs={{0,1},{1,0},{2,3},{3,2},{4,5},{5,4},{6,7},{7,6},{8,9},{9,8},{10,11... | collective-permute-start | bytes 18440 | tf_op jit(solution)/shard_map/ppermute | solution.py:406
  193.5 9.9 %collective-permute-start.33 = (bf16[384,512]{1,0:T(8,128)(2,1)S(1)}, bf16[384,512]{1,0:T(8,128)(2,1)S(1)}, u32[]{:S(2)}, u32[]{:S(2)}) collective-permute-start(bf16[384,512]{1,0:T(8,128)(2,1)S(1)} %slice_select_fusion), channel_id=1, source_target_pairs={{0,2},{3,1},{4,6},{7,5},{8,10},{11,9},{12,14},{15,13},{16,18},{19,... | collective-permute-start | bytes 1179656 | tf_op jit(solution)/shard_map/ppermute | solution.py:380
  196.1 10.3 %collective-permute-start.32 = (bf16[384,512]{1,0:T(8,128)(2,1)S(1)}, bf16[384,512]{1,0:T(8,128)(2,1)S(1)}, u32[]{:S(2)}, u32[]{:S(2)}) collective-permute-start(bf16[384,512]{1,0:T(8,128)(2,1)S(1)} %get-tuple-element.119), channel_id=1, source_target_pairs={{2,0},{1,3},{6,4},{5,7},{10,8},{9,11},{14,12},{13,15},{18,16},{17,... | collective-permute-start | bytes 1179656 | tf_op jit(solution)/shard_map/ppermute | solution.py:380
  199.1 10.8 %collective-permute-start.39 = (f32[2,384]{1,0:T(2,128)S(1)}, f32[2,384]{1,0:T(2,128)S(1)}, u32[]{:S(2)}, u32[]{:S(2)}) collective-permute-start(f32[2,384]{1,0:T(2,128)S(1)} %pad_maximum_fusion.10), channel_id=1, source_target_pairs={{4,0},{8,12},{5,1},{9,13},{6,2},{10,14},{7,3},{11,15},{20,16},{24,... | collective-permute-start | bytes 9224 | tf_op jit(solution)/shard_map/ppermute | solution.py:420
  (12 other events, 31.5 us)
